TPU v7x, 256 devices: a whole 4x4x8 slice. The times are simulated.
256 devices in a mesh: band: 32 (over x, z_lo, core), dom: 8 (over y, z_hi).
Axes of the slice: x: 4, y: 4, z: 8 (z_hi: 2, z_lo: 4; z = z_hi * 4 + z_lo), core: 2. Of those that a mesh axis runs over, the one named last changes fastest.
Arguments:
- orbitals: bfloat16 [96, 64, 8192], P('dom', None, 'band'), may hold values from -19 to 19
- potential: bfloat16 [96, 64], replicated, may hold values from -1 to 0
- rot_first: bfloat16 [8192, 8192], P('dom', 'band'), may hold values from -0.0625 to 0.0625
- rot_second: bfloat16 [8192, 8192], P('dom', 'band'), may hold values from -0.0625 to 0.0625
Outputs:
- rotated: bfloat16 [96, 64, 8192], P('dom', None, 'band')
All inputs are finite; a program needn't handle non-finite values.
Results may differ from a plain program's by a relative error of at most 0.0063.
Values may be sent and summed in bfloat16 or wider, within the bound.
A program may use at most 64 MiB of HBM per device.

v0:
```python
import jax
import jax.numpy as jnp
from jax import lax
from jax.sharding import PartitionSpec as P

stencil_weights = (
    -5369.0 / 1800.0,
    12.0 / 7.0,
    -15.0 / 56.0,
    10.0 / 189.0,
    -1.0 / 112.0,
    2.0 / 1925.0,
    -1.0 / 16632.0,
)
filter_center = 3.8
filter_half = 3.3


def with_halo(shard, sides, width):
    for axis, dim in sides:
        size, length = (lax.axis_size(axis), shard.shape[dim])
        up = [(i, (i + 1) % size) for i in range(size - 1)]
        down = [(j, i) for i, j in up]
        last = lax.slice_in_dim(shard, length - width, length, axis=dim)
        initial = lax.slice_in_dim(shard, 0, width, axis=dim)
        before = lax.ppermute(last, axis, up)
        after = lax.ppermute(initial, axis, down)
        shard = jnp.concatenate([before, shard, after], axis=dim)
    return shard


def hamiltonian(padded, volts):
    wide = padded.astype(jnp.float32)
    width = wide.shape[0] - 12
    height = wide.shape[1]
    center = wide[6 : 6 + width]
    ypadded = jnp.pad(center, ((0, 0), (6, 6), (0, 0)))
    lap = 2.0 * stencil_weights[0] * center
    for offset in range(1, 7):
        lap = lap + stencil_weights[offset] * (
            wide[6 + offset : 6 + offset + width]
            + wide[6 - offset : 6 - offset + width]
            + ypadded[:, 6 + offset : 6 + offset + height]
            + ypadded[:, 6 - offset : 6 - offset + height]
        )
    return (-0.5 * lap + volts[:, :, None] * center, center)


def first_step(padded, volts):
    applied, center = hamiltonian(padded, volts)
    return ((applied - filter_center * center) / filter_half).astype(jnp.bfloat16)


def second_step(padded, volts, start):
    applied, center = hamiltonian(padded, volts)
    return (2.0 * (applied - filter_center * center) / filter_half - start).astype(jnp.bfloat16)


def rotate(flat, coeffs):
    everything = lax.all_gather(flat, "band", axis=1, tiled=True)
    return jnp.dot(everything, coeffs, preferred_element_type=jnp.float32)


def shards(orbitals, potential, rot_first, rot_second):
    columns = orbitals.shape[0]
    height = orbitals.shape[1]
    width = orbitals.shape[2]
    coef_first, coef_second = (
        lax.all_gather(rot_first, "dom", axis=0, tiled=True),
        lax.all_gather(rot_second, "dom", axis=0, tiled=True),
    )
    first_column = lax.axis_index("dom") * columns
    grid_columns = columns * lax.axis_size("dom")
    volt_pad = jnp.pad(potential.astype(jnp.float32), ((12, 12), (0, 0)))
    volts_own = lax.dynamic_slice_in_dim(volt_pad, first_column + 12, columns, 0)
    start = orbitals.astype(jnp.float32)

    def with_rim(field):
        return with_halo(field, (("dom", 0),), 6)

    first_degree = first_step(with_rim(orbitals), volts_own)
    filtered = second_step(with_rim(first_degree), volts_own, start)
    flat = filtered.reshape(columns * height, width)
    turned = rotate(flat, coef_first)
    squares = lax.psum(jnp.sum(turned * turned, axis=0), "dom")
    mean_square = squares / (grid_columns * height)
    normed = (turned / jnp.sqrt(mean_square + 1e-06)[None, :]).astype(jnp.bfloat16)
    rotated = rotate(normed, coef_second).astype(jnp.bfloat16)
    return rotated.reshape(columns, height, width)


def solution(mesh):
    placed = (P("dom", None, "band"), P(), P("dom", "band"), P("dom", "band"))
    return jax.shard_map(
        shards, mesh=mesh, in_specs=placed, out_specs=P("dom", None, "band"), check_vma=False
    )
```

profile of v0, /device:TPU:1, one launch (start us, length us, event | category | flops | bytes accessed | tf_op | source)
XLA Modules:
  0.0 466.1 jit_solution(12350468299757759940)
XLA Ops:
  6.5 0.0 all-gather.7.cloned.1.call-start
  6.5 0.7 all-gather.7.cloned.1.call-update
  7.3 0.0 all-gather.5.cloned.1.call-start
  7.3 1.1 fusion.60
  8.4 9.7 %collective-permute-start = (bf16[6,64,256]{2,1,0:T(8,128)(2,1)S(1)}, bf16[6,64,256]{2,1,0:T(8,128)(2,1)S(1)}, u32[]{:S(2)}, u32[]{:S(2)}) collective-permute-start(bf16[6,64,256]{2,1,0:T(8,128)(2,1)S(1)} %get-tuple-element.7), channel_id=1, source_target_pairs={{0,1},{1,2},{2,3},{3,4},{4,5},{5,6},{6,7},{8,9},{9,10},{10,11},{11... | collective-permute-start | bytes 589832 | tf_op jit(solution)/shard_map/ppermute | solution.py:26
  18.0 1.3 collective-permute-start.1
  19.3 0.8 dynamic-slice_convert_fusion
  20.1 0.1 copy.5
  20.2 1.6 collective-permute-done
  21.8 10.7 %collective-permute-done.1 = bf16[6,64,256]{2,1,0:T(8,128)(2,1)S(1)} collective-permute-done((bf16[6,64,256]{2,1,0:T(8,128)(2,1)S(1)}, bf16[6,64,256]{2,1,0:T(8,128)(2,1)S(1)}, u32[]{:S(2)}, u32[]{:S(2)}) %collective-permute-start.1) | collective-permute-done | bytes 196640 | tf_op jit(solution)/shard_map/ppermute | solution.py:27
  32.5 1.1 maximum_convert_fusion
  33.6 0.1 slice.216
  33.7 1.7 fusion.57
  35.4 0.0 copy-start
  35.5 13.3 %collective-permute-start.2 = (bf16[6,64,256]{2,1,0:T(8,128)(2,1)S(1)}, bf16[6,64,256]{2,1,0:T(8,128)(2,1)S(1)}, u32[]{:S(2)}, u32[]{:S(2)}) collective-permute-start(bf16[6,64,256]{2,1,0:T(8,128)(2,1)S(1)} %get-tuple-element.5), channel_id=1, source_target_pairs={{0,1},{1,2},{2,3},{3,4},{4,5},{5,6},{6,7},{8,9},{9,10},{10,11},{11... | collective-permute-start | bytes 589832 | tf_op jit(solution)/shard_map/ppermute | solution.py:26
  48.8 1.3 collective-permute-start.3
  50.1 1.3 collective-permute-done.2
  51.4 13.9 %collective-permute-done.3 = bf16[6,64,256]{2,1,0:T(8,128)(2,1)S(1)} collective-permute-done((bf16[6,64,256]{2,1,0:T(8,128)(2,1)S(1)}, bf16[6,64,256]{2,1,0:T(8,128)(2,1)S(1)}, u32[]{:S(2)}, u32[]{:S(2)}) %collective-permute-start.3) | collective-permute-done | bytes 196640 | tf_op jit(solution)/shard_map/ppermute | solution.py:27
  65.3 0.1 maximum_convert_fusion.1
  65.4 0.1 slice.231
  65.5 0.0 copy-done
  65.5 2.5 fusion.58
  68.0 0.0 all-gather.5.cloned.1.call-update
  68.0 0.0 all-gather.11.cloned.1.call-start
  68.1 0.7 all-gather.11.cloned.1.call-update
  68.8 0.0 all-gather.9.cloned.1.call-start
  68.8 65.8 %all-gather.7.cloned.1.call-done = bf16[8192,256]{1,0:T(8,128)(2,1)} async-done(((bf16[1024,256]{1,0:T(8,128)(2,1)}), bf16[8192,256]{1,0:T(8,128)(2,1)}) %all-gather.7.cloned.1.call-update) | async-done | bytes 4194320 | tf_op jit(solution)/shard_map/all_gather | solution.py:69
  134.6 105.5 %all-gather.5.cloned.1.call-done = bf16[768,8192]{1,0:T(8,128)(2,1)} async-done(((bf16[768,256]{1,0:T(8,128)(2,1)}), bf16[768,8192]{1,0:T(8,128)(2,1)}) %all-gather.5.cloned.1.call-update) | async-done | bytes 12582928 | tf_op jit(solution)/shard_map/all_gather | solution.py:60
  240.2 7.6 %multiply_reduce_fusion = (f32[256]{0:T(256)S(1)}, f32[768,256]{1,0:T(8,128)S(1)}) fusion(bf16[768,8192]{1,0:T(8,128)(2,1)} %all-gather.5.cloned.1.call-done, bf16[8192,256]{1,0:T(8,128)(2,1)} %all-gather.7.cloned.1.call-done), kind=kOutput, calls=%fused_computation.97 | convolution fusion | flops 3221618432 | bytes 17564672 | tf_op jit(solution)/shard_map/dot_general | solution.py:61
  247.8 25.9 %psum.7 = f32[256]{0:T(256)S(1)} all-reduce(f32[256]{0:T(256)S(1)} %get-tuple-element.9), channel_id=1, replica_groups=mesh['band'=32,'dom'=8] {'dom'}, use_global_device_ids=true, to_apply=%region_1.2 | all-reduce | flops 256 | bytes 2048 | tf_op jit(solution)/shard_map/psum | solution.py:85
  273.7 0.8 divide_convert_fusion
  274.6 0.0 all-gather.9.cloned.1.call-update
  274.6 72.5 %all-gather.11.cloned.1.call-done = bf16[8192,256]{1,0:T(8,128)(2,1)} async-done(((bf16[1024,256]{1,0:T(8,128)(2,1)}), bf16[8192,256]{1,0:T(8,128)(2,1)}) %all-gather.11.cloned.1.call-update) | async-done | bytes 4194320 | tf_op jit(solution)/shard_map/all_gather | solution.py:70
  347.1 102.6 %all-gather.9.cloned.1.call-done = bf16[768,8192]{1,0:T(8,128)(2,1)} async-done(((bf16[768,256]{1,0:T(8,128)(2,1)}), bf16[768,8192]{1,0:T(8,128)(2,1)}) %all-gather.9.cloned.1.call-update) | async-done | bytes 12582928 | tf_op jit(solution)/shard_map/all_gather | solution.py:60
  449.7 9.9 %convolution_convert_fusion = bf16[768,256]{1,0:T(8,128)(2,1)} fusion(bf16[768,8192]{1,0:T(8,128)(2,1)} %all-gather.9.cloned.1.call-done, bf16[8192,256]{1,0:T(8,128)(2,1)} %all-gather.11.cloned.1.call-done), kind=kOutput, calls=%fused_computation.24 | convolution fusion | flops 3221422080 | bytes 17170432 | tf_op jit(solution)/shard_map/dot_general | solution.py:61
  (2 shorter events, 0.0 us)
Async XLA Ops:
  6.5 128.1 %all-gather.7.cloned.1.call-start = ((), (), s32[]{:S(2)}) async-start(), calls=%async_computation.1 | async-start | bytes 4718592 | tf_op jit(solution)/shard_map/all_gather | solution.py:69
  7.3 232.9 %all-gather.5.cloned.1.call-start = ((), (), s32[]{:S(2)}) async-start(), calls=%async_computation | async-start | bytes 12976128 | tf_op jit(solution)/shard_map/all_gather | solution.py:60
  8.4 13.4 %collective-permute-start = (bf16[6,64,256]{2,1,0:T(8,128)(2,1)S(1)}, bf16[6,64,256]{2,1,0:T(8,128)(2,1)S(1)}, u32[]{:S(2)}, u32[]{:S(2)}) collective-permute-start(bf16[6,64,256]{2,1,0:T(8,128)(2,1)S(1)} %get-tuple-element.7), channel_id=1, source_target_pairs={{0,1},{1,2},{2,3},{3,4},{4,5},{5,6},{6,7},{8,9},{9,10},{10,11},{11... | collective-permute-start | bytes 589832 | tf_op jit(solution)/shard_map/ppermute | solution.py:26
  18.0 14.5 %collective-permute-start.1 = (bf16[6,64,256]{2,1,0:T(8,128)(2,1)S(1)}, bf16[6,64,256]{2,1,0:T(8,128)(2,1)S(1)}, u32[]{:S(2)}, u32[]{:S(2)}) collective-permute-start(bf16[6,64,256]{2,1,0:T(8,128)(2,1)S(1)} %get-tuple-element.8), channel_id=1, source_target_pairs={{1,0},{2,1},{3,2},{4,3},{5,4},{6,5},{7,6},{9,8},{10,9},{11,10},{12... | collective-permute-start | bytes 589832 | tf_op jit(solution)/shard_map/ppermute | solution.py:27
  35.4 30.1 %copy-start = (bf16[12,64,256]{2,1,0:T(8,128)(2,1)S(1)}, bf16[12,64,256]{2,1,0:T(8,128)(2,1)}, u32[]{:S(2)}) copy-start(bf16[12,64,256]{2,1,0:T(8,128)(2,1)} %param.4) | copy-start | bytes 1179652
  35.5 15.9 %collective-permute-start.2 = (bf16[6,64,256]{2,1,0:T(8,128)(2,1)S(1)}, bf16[6,64,256]{2,1,0:T(8,128)(2,1)S(1)}, u32[]{:S(2)}, u32[]{:S(2)}) collective-permute-start(bf16[6,64,256]{2,1,0:T(8,128)(2,1)S(1)} %get-tuple-element.5), channel_id=1, source_target_pairs={{0,1},{1,2},{2,3},{3,4},{4,5},{5,6},{6,7},{8,9},{9,10},{10,11},{11... | collective-permute-start | bytes 589832 | tf_op jit(solution)/shard_map/ppermute | solution.py:26
  48.8 16.5 %collective-permute-start.3 = (bf16[6,64,256]{2,1,0:T(8,128)(2,1)S(1)}, bf16[6,64,256]{2,1,0:T(8,128)(2,1)S(1)}, u32[]{:S(2)}, u32[]{:S(2)}) collective-permute-start(bf16[6,64,256]{2,1,0:T(8,128)(2,1)S(1)} %get-tuple-element.6), channel_id=1, source_target_pairs={{1,0},{2,1},{3,2},{4,3},{5,4},{6,5},{7,6},{9,8},{10,9},{11,10},{12... | collective-permute-start | bytes 589832 | tf_op jit(solution)/shard_map/ppermute | solution.py:27
  68.0 279.1 %all-gather.11.cloned.1.call-start = ((), (), s32[]{:S(2)}) async-start(), calls=%async_computation.3 | async-start | bytes 4718592 | tf_op jit(solution)/shard_map/all_gather | solution.py:70
  68.8 380.9 %all-gather.9.cloned.1.call-start = ((), (), s32[]{:S(2)}) async-start(), calls=%async_computation.2 | async-start | bytes 12976128 | tf_op jit(solution)/shard_map/all_gather | solution.py:60
Sparse Core Ops, SparseCore 0:
  10.0 124.5 all-gather.6
  136.4 103.7 all-gather.4
  242.8 104.2 all-gather.10
  348.7 100.9 all-gather.8
where the time goes:
time: 466 us
  waiting for transfers between devices  375 us (80%)
  blocking collectives  25.9 us (6%)
  starting transfers between devices  25.7 us (6%)
  matrix products  17.6 us (4%)
  between operations  13.2 us (3%)
  other arithmetic  7.11 us (2%)
    all_gather x2, waiting for transfers between devices, rotate(): everything = lax.all_gather(flat, 'band', axis=1, tiled=True)  208 us
    all_gather x1, waiting for transfers between devices, shards(): lax.all_gather(rot_second, 'dom', axis=0, tiled=True)  72.5 us
    all_gather x1, waiting for transfers between devices, shards(): lax.all_gather(rot_first, 'dom', axis=0, tiled=True)  65.8 us
    psum x1, blocking collectives, shards(): squares = lax.psum(jnp.sum(turned * turned, axis=0), 'dom')  25.9 us
    ppermute x2, waiting for transfers between devices, with_halo(): after = lax.ppermute(initial, axis, down)  24.6 us
    ppermute x2, starting transfers between devices, with_halo(): before = lax.ppermute(last, axis, up)  23 us
    dot_general x2, matrix products, rotate(): return jnp.dot(everything, coeffs, preferred_element_type=jnp.float32)  17.6 us
  transfers between devices with their start and end apart: 8, of which 8 were waited for; matrix products, arithmetic and copies ran while one was open for 3% of the time, Pallas kernels for 0%

commit v1 on v0

v1 whole, which is shorter than its diff:
```python
import functools

import jax
import jax.numpy as jnp
from jax import lax
from jax.experimental import pallas as pl
from jax.experimental.pallas import tpu as pltpu
from jax.sharding import PartitionSpec as P

stencil_weights = (
    -5369.0 / 1800.0,
    12.0 / 7.0,
    -15.0 / 56.0,
    10.0 / 189.0,
    -1.0 / 112.0,
    2.0 / 1925.0,
    -1.0 / 16632.0,
)
filter_center = 3.8
filter_half = 3.3

MESH = pl.DeviceIdType.MESH
GRID_X = 96
NY = 64
OWN = 12
ROWS = OWN * NY
LANES = 256
HALF = 128
CHUNKS = 3
CROWS = ROWS // CHUNKS
PAIR = 2 * OWN
EXT = PAIR + 12
CELLS = GRID_X * NY


def aligned(value, multiple):
    return pl.multiple_of(value, multiple)


def kernel(
    orb, pot, r1, r2, out,
    oext, dext, vpad, volt, filt, g1, g2, rb1, rb2, pbuf, prec, tq, sq,
    swap_s, swap_r, back_s, back_r, loc, halo_s, halo_r,
    g_s, g_r, p_s, p_r, sq_s, sq_r, rz_s, rz_r, ry_s, ry_r,
):
    band = lax.axis_index("band")
    dom = lax.axis_index("dom")
    x = band // 8
    zl = (band // 2) % 4
    za = zl // 2
    zb = zl % 2
    core = band % 2
    y = dom // 2
    zh = dom % 2

    def device(x_=None, y_=None, zh_=None, za_=None, zb_=None, core_=None):
        pick = lambda new, old: old if new is None else new
        b = pick(x_, x) * 8 + (pick(za_, za) * 2 + pick(zb_, zb)) * 2 + pick(core_, core)
        d = pick(y_, y) * 2 + pick(zh_, zh)
        return {"band": b, "dom": d}

    def around(value, step):
        return (value + step) % 4

    def remote(src, dst, send, recv, to):
        return pltpu.make_async_remote_copy(
            src_ref=src, dst_ref=dst, send_sem=send, recv_sem=recv, device_id=to, device_id_type=MESH
        )

    barrier = pltpu.get_barrier_semaphore()
    partners = []
    for step in range(1, 8):
        z = (zh * 4 + zl + step) % 8
        partners.append(device(zh_=z // 4, za_=(z // 2) % 2, zb_=z % 2))
    for step in range(1, 4):
        partners.append(device(x_=around(x, step)))
        partners.append(device(y_=around(y, step)))
        partners.append(device(y_=around(y, step), zh_=1 - zh))
    partners.append(device(core_=1 - core))
    for to in partners:
        pl.semaphore_signal(barrier, inc=1, device_id=to, device_id_type=MESH)
    pl.semaphore_wait(barrier, len(partners))

    mine = aligned(zh * HALF, HALF)
    theirs = aligned((1 - zh) * HALF, HALF)
    own_at = aligned((6 + OWN * zh) * NY, NY)
    partner_at = aligned((6 + OWN * (1 - zh)) * NY, NY)
    swap = remote(
        orb.at[:, pl.ds(theirs, HALF)], oext.at[pl.ds(own_at, ROWS)], swap_s, swap_r, device(zh_=1 - zh)
    )
    swap.start()
    keep = pltpu.make_async_copy(orb.at[:, pl.ds(mine, HALF)], oext.at[pl.ds(own_at, ROWS)], loc.at[0])
    keep.start()

    def coef_z(i, r, rb):
        rows = pl.ds(aligned(y * 1024, 1024), 1024)
        here = rb.at[za, rows]
        other = remote(r, here, rz_s.at[i, 0], rz_r.at[i, za], device(zh_=1 - zh, za_=zh))
        near = remote(r, here, rz_s.at[i, 1], rz_r.at[i, za], device(za_=zh))
        own = pltpu.make_async_copy(r, here, rz_r.at[i, za])
        return other, near, own

    def coef_z_start(i, r, rb):
        other, near, own = coef_z(i, r, rb)
        other.start()

        @pl.when(za != zh)
        def _():
            near.start()

        @pl.when(za == zh)
        def _():
            own.start()

    def coef_y(i, rb, part):
        rows = pl.ds(aligned(y * 1024, 1024), 1024)
        return [
            remote(
                rb.at[part, rows], rb.at[part, rows], ry_s.at[i, part, step - 1], ry_r.at[i, part, step - 1],
                device(y_=around(y, step)),
            )
            for step in (1, 3, 2)
        ]

    def coef_y_start(i, r, rb):
        for part in range(2):
            pltpu.make_async_copy(r, rb.at[part, pl.ds(aligned(y * 1024, 1024), 1024)], rz_r.at[i, part]).wait()
            for copy in coef_y(i, rb, part):
                copy.start()

    def coef_wait(i, rb):
        for part in range(2):
            for copy in coef_y(i, rb, part):
                copy.wait_recv()

    def coef_end(i, r, rb):
        other, near, own = coef_z(i, r, rb)
        other.wait_send()

        @pl.when(za != zh)
        def _():
            near.wait_send()

        for part in range(2):
            for copy in coef_y(i, rb, part):
                copy.wait_send()

    coef_z_start(0, r1, rb1)

    diagonal = lax.broadcasted_iota(jnp.int32, (NY, NY), 0) == lax.broadcasted_iota(jnp.int32, (NY, NY), 1)
    ones = jnp.ones((NY, HALF), jnp.bfloat16)

    def spread(i, carry):
        row = pot[pl.ds(y * PAIR + i, 1), :]
        square = jnp.where(diagonal, jnp.broadcast_to(row, (NY, NY)), 0.0).astype(jnp.bfloat16)
        volt[i] = jnp.dot(square, ones, preferred_element_type=jnp.float32)
        return carry

    lax.fori_loop(0, PAIR, spread, 0)

    def clear(i, carry):
        vpad[i, 0:8, :] = jnp.zeros((8, HALF), jnp.float32)
        vpad[i, 72:80, :] = jnp.zeros((8, HALF), jnp.float32)
        return carry

    lax.fori_loop(0, EXT, clear, 0)

    def rims(i, ext):
        up = remote(
            ext.at[pl.ds(24 * NY, 6 * NY)], ext.at[pl.ds(0, 6 * NY)], halo_s.at[i, 0], halo_r.at[i, 0],
            device(y_=around(y, 1)),
        )
        down = remote(
            ext.at[pl.ds(6 * NY, 6 * NY)], ext.at[pl.ds(30 * NY, 6 * NY)], halo_s.at[i, 1], halo_r.at[i, 1],
            device(y_=around(y, 3)),
        )
        return up, down

    def widen(ext, first, count, keep_it):
        def step(i, carry):
            at = first + i
            value = ext[pl.ds(aligned(at * NY, NY), NY), :].astype(jnp.float32)
            if keep_it is not None:
                value = jnp.where(keep_it, value, 0.0)
            vpad[at, 8:72, :] = value
            return carry

        lax.fori_loop(0, count, step, 0)

    def applied(i):
        center = vpad[i + 6, 8:72, :]
        lap = 2.0 * stencil_weights[0] * center
        for k in range(1, 7):
            lap = lap + stencil_weights[k] * (
                (vpad[i + 6 + k, 8:72, :] + vpad[i + 6 - k, 8:72, :])
                + (vpad[i + 6, 8 + k : 72 + k, :] + vpad[i + 6, 8 - k : 72 - k, :])
            )
        return -0.5 * lap + volt[i] * center, center

    def field(i, ext):
        for copy in rims(i, ext):
            copy.start()
        widen(ext, 6, PAIR, None)
        for copy in rims(i, ext):
            copy.wait_recv()
        widen(ext, 0, 6, y > 0)
        widen(ext, 30, 6, y < 3)

    keep.wait()
    swap.wait_recv()
    field(0, oext)

    def first(i, carry):
        value, center = applied(i)
        dext[pl.ds(aligned((i + 6) * NY, NY), NY), :] = (
            (value - filter_center * center) * (1.0 / filter_half)
        ).astype(jnp.bfloat16)
        return carry

    lax.fori_loop(0, PAIR, first, 0)
    field(1, dext)

    def second(i, carry):
        value, center = applied(i)
        start = oext[pl.ds(aligned((i + 6) * NY, NY), NY), :].astype(jnp.float32)
        filt[pl.ds(aligned(i * NY, NY), NY), :] = (
            (value - filter_center * center) * (2.0 / filter_half) - start
        ).astype(jnp.bfloat16)
        return carry

    own_slot = (x * 2 + zb) * 2 + core
    half_lanes = pl.ds(mine, HALF)

    def back(j):
        source = filt.at[pl.ds(aligned((1 - zh) * ROWS + j * CROWS, CROWS), CROWS)]
        place = g1.at[own_slot, pl.ds(j * CROWS, CROWS), half_lanes]
        return remote(source, place, back_s.at[j], back_r.at[j], device(zh_=1 - zh))

    def stay(j):
        source = filt.at[pl.ds(aligned(zh * ROWS + j * CROWS, CROWS), CROWS)]
        place = g1.at[own_slot, pl.ds(j * CROWS, CROWS), half_lanes]
        return pltpu.make_async_copy(source, place, loc.at[1 + j])

    per = OWN // CHUNKS
    for j in range(CHUNKS):
        lax.fori_loop((1 - zh) * OWN + j * per, (1 - zh) * OWN + (j + 1) * per, second, 0)
        back(j).start()
    for j in range(CHUNKS):
        lax.fori_loop(zh * OWN + j * per, zh * OWN + (j + 1) * per, second, 0)
        stay(j).start()

    other_core = device(core_=1 - core)

    def block(g, slot, j):
        return g.at[slot, pl.ds(aligned(j * CROWS, CROWS), CROWS)]

    def send(i, g, slot, j, n, to):
        return remote(block(g, slot, j), block(g, slot, j), g_s.at[i, j, n], g_r.at[i, j, slot], to)

    def own_sends(i, g, j):
        places = [device(zb_=1 - zb), device(x_=around(x, 1)), device(x_=around(x, 3)), device(x_=around(x, 2)), other_core]
        return [send(i, g, own_slot, j, n, to) for n, to in enumerate(places)]

    def pair_sends(i, g, j):
        slot = (x * 2 + 1 - zb) * 2 + core
        places = [device(x_=around(x, 1)), device(x_=around(x, 3)), device(x_=around(x, 2)), other_core]
        return [send(i, g, slot, j, 5 + n, to) for n, to in enumerate(places)]

    def far_sends(i, g, j):
        sends = []
        for step in (1, 3, 2):
            for b in (0, 1):
                slot = (around(x, step) * 2 + b) * 2 + core
                sends.append(send(i, g, slot, j, 9 + len(sends), other_core))
        return sends

    def arrived(i, g, slot, j):
        send(i, g, slot, j, 0, other_core).wait_recv()

    def gather_own(i, g, j):
        for copy in own_sends(i, g, j):
            copy.start()

    def gather_pair(i, g, j):
        arrived(i, g, (x * 2 + 1 - zb) * 2 + core, j)
        for copy in pair_sends(i, g, j):
            copy.start()

    def gather_far(i, g, j):
        for copy in far_sends(i, g, j):
            copy.wait_recv()
            copy.start()
        for slot in range(8):
            arrived(i, g, slot * 2 + 1 - core, j)

    def gather_end(i, g):
        def step(j, carry):
            for copy in own_sends(i, g, j) + pair_sends(i, g, j) + far_sends(i, g, j):
                copy.wait_send()
            return carry

        lax.fori_loop(0, CHUNKS, step, 0)

    def product(g, rb, j, part):
        rows = pl.ds(aligned(j * CROWS, CROWS), CROWS)
        total = None
        for slot in range(16):
            term = jnp.dot(
                g[slot, rows, :], rb[part, slot * LANES : (slot + 1) * LANES, :], preferred_element_type=jnp.float32
            )
            total = term if total is None else total + term
        return total

    def partial_send(i, j):
        return remote(pbuf.at[i, j], prec.at[i, j], p_s.at[i, j], p_r.at[i, j], device(za_=1 - za))

    def rotate(i, g, rb):
        def step(j, carry):
            gather_far(i, g, j)
            pbuf[i, j] = product(g, rb, j, 1 - za).astype(jnp.bfloat16)
            partial_send(i, j).start()
            tq[j] = product(g, rb, j, za)
            return carry

        lax.fori_loop(0, CHUNKS, step, 0)

    coef_y_start(0, r1, rb1)
    coef_z_start(1, r2, rb2)
    for j in range(CHUNKS):
        stay(j).wait()
        back(j).wait_recv()
        gather_own(0, g1, j)
    for j in range(CHUNKS):
        gather_pair(0, g1, j)
    coef_wait(0, rb1)
    rotate(0, g1, rb1)
    coef_y_start(1, r2, rb2)

    sums = jnp.zeros((8, LANES), jnp.float32)
    for j in range(CHUNKS):
        partial_send(0, j).wait_recv()

        def squares(n, total):
            rows = pl.ds(aligned(n * 32, 32), 32)
            value = tq[j, rows, :] + prec[0, j, rows, :].astype(jnp.float32)
            tq[j, rows, :] = value
            return total + jnp.sum((value * value).reshape(4, 8, LANES), axis=0)

        sums = lax.fori_loop(0, CROWS // 32, squares, sums)
    sq[dom] = sums

    def share(step):
        to = (dom + step) % 8
        return remote(sq.at[dom], sq.at[dom], sq_s.at[step - 1], sq_r.at[step - 1], {"band": band, "dom": to})

    for step in range(1, 8):
        share(step).start()
    for step in range(1, 8):
        share(step).wait_recv()
    total = sq[0]
    for d in range(1, 8):
        total = total + sq[d]
    mean_square = jnp.sum(total, axis=0, keepdims=True) * (1.0 / CELLS)
    scale = 1.0 / jnp.sqrt(mean_square + 1e-06)
    for j in range(CHUNKS):

        def normalize(n, carry):
            rows = pl.ds(aligned(n * 32, 32), 32)
            g2[own_slot, pl.ds(aligned(j * CROWS + n * 32, 32), 32), :] = (tq[j, rows, :] * scale).astype(jnp.bfloat16)
            return carry

        lax.fori_loop(0, CROWS // 32, normalize, 0)
        gather_own(1, g2, j)

    for j in range(CHUNKS):
        gather_pair(1, g2, j)
    coef_wait(1, rb2)
    rotate(1, g2, rb2)

    for j in range(CHUNKS):
        partial_send(1, j).wait_recv()

        def finish(n, carry):
            rows = pl.ds(aligned(n * 32, 32), 32)
            out[pl.ds(aligned(j * CROWS + n * 32, 32), 32), :] = (
                tq[j, rows, :] + prec[1, j, rows, :].astype(jnp.float32)
            ).astype(jnp.bfloat16)
            return carry

        lax.fori_loop(0, CROWS // 32, finish, 0)

    swap.wait_send()
    for j in range(CHUNKS):
        back(j).wait_send()
    for i, ext in ((0, oext), (1, dext)):
        for copy in rims(i, ext):
            copy.wait_send()
    for i, (g, r, rb) in enumerate(((g1, r1, rb1), (g2, r2, rb2))):
        gather_end(i, g)
        coef_end(i, r, rb)
        for j in range(CHUNKS):
            partial_send(i, j).wait_send()
    for step in range(1, 8):
        share(step).wait_send()


def shards(orbitals, potential, rot_first, rot_second):
    bf16, f32 = jnp.bfloat16, jnp.float32
    vmem = pl.BlockSpec(memory_space=pltpu.VMEM)
    dma = pltpu.SemaphoreType.DMA
    result = pl.pallas_call(
        kernel,
        out_shape=jax.ShapeDtypeStruct((ROWS, LANES), bf16),
        in_specs=[vmem] * 4,
        out_specs=vmem,
        scratch_shapes=[
            pltpu.VMEM((EXT * NY, HALF), bf16),
            pltpu.VMEM((EXT * NY, HALF), bf16),
            pltpu.VMEM((EXT, NY + 16, HALF), f32),
            pltpu.VMEM((PAIR, NY, HALF), f32),
            pltpu.VMEM((PAIR * NY, HALF), bf16),
            pltpu.VMEM((16, ROWS, LANES), bf16),
            pltpu.VMEM((16, ROWS, LANES), bf16),
            pltpu.VMEM((2, 4096, LANES), bf16),
            pltpu.VMEM((2, 4096, LANES), bf16),
            pltpu.VMEM((2, CHUNKS, CROWS, LANES), bf16),
            pltpu.VMEM((2, CHUNKS, CROWS, LANES), bf16),
            pltpu.VMEM((CHUNKS, CROWS, LANES), f32),
            pltpu.VMEM((8, 8, LANES), f32),
            dma, dma,
            dma((CHUNKS,)), dma((CHUNKS,)),
            dma((1 + CHUNKS,)),
            dma((2, 2)), dma((2, 2)),
            dma((2, CHUNKS, 15)), dma((2, CHUNKS, 16)),
            dma((2, CHUNKS)), dma((2, CHUNKS)),
            dma((7,)), dma((7,)),
            dma((2, 2)), dma((2, 2)),
            dma((2, 2, 3)), dma((2, 2, 3)),
        ],
        compiler_params=pltpu.CompilerParams(
            collective_id=0, has_side_effects=True, vmem_limit_bytes=56 << 20
        ),
    )(orbitals.reshape(ROWS, LANES), potential.astype(f32), rot_first, rot_second)
    return result.reshape(OWN, NY, LANES)


def solution(mesh):
    placed = (P("dom", None, "band"), P(), P("dom", "band"), P("dom", "band"))
    return jax.shard_map(
        shards, mesh=mesh, in_specs=placed, out_specs=P("dom", None, "band"), check_vma=False
    )
```

time: 466 us -> 226 us (0.48)
  waiting for transfers between devices: 375 us -> 0 us
  Pallas kernels: 0 us -> 223 us
  blocking collectives: 25.9 us -> 0 us
  starting transfers between devices: 25.7 us -> 0 us
  matrix products: 17.6 us -> 0 us
  between operations: 13.2 us -> 0.01 us
  other arithmetic: 7.11 us -> 0 us
    all_gather x4 -> x0, waiting for transfers between devices: 346 us -> none  [the longest x2 208 us: rotate(): everything = lax.all_gather(flat, 'band', axis=1, tiled=True)]
    pallas_call x0 -> x1, Pallas kernels: none -> 223 us  [shards(): pl.pallas_call(kernel, out_shape=jax.ShapeDtypeStruct((ROWS, LANES), bf16...]
    ppermute x4 -> x0, waiting for transfers between devices: 27.5 us -> none  [the longest x2 24.6 us: with_halo(): after = lax.ppermute(initial, axis, down)]
    psum x1 -> x0, blocking collectives: 25.9 us -> none  [shards(): squares = lax.psum(jnp.sum(turned * turned, axis=0), 'dom')]
    ppermute x4 -> x0, starting transfers between devices: 25.6 us -> none  [the longest x2 23 us: with_halo(): before = lax.ppermute(last, axis, up)]
    dot_general x2 -> x0, matrix products: 17.6 us -> none  [rotate(): return jnp.dot(everything, coeffs, preferred_element_type=jnp.float32)]
    convert_element_type x5 -> x0, other arithmetic: 6.29 us -> none  [the longest x1 2.5 us: second_step(): (2.0 * (applied - filter_center * center) / filter_half - start).astype(j...]
  transfers between devices with their start and end apart: 8 -> 0, of which waited for: 8 -> 0; matrix products, arithmetic and copies ran while one was open for 3% -> 0% of each run, Pallas kernels for 0% -> 0%
where the time goes in v1:
time: 226 us
  Pallas kernels  223 us (99%)
  local copies, waits for them, and re-layouts  3.2 us (1%)
    pallas_call x1, Pallas kernels, shards(): pl.pallas_call(kernel, out_shape=jax.ShapeDtypeStruct((ROWS, LANES), bf16...  223 us

profile of v1, /device:TPU:1, one launch (start us, length us, event | category | flops | bytes accessed | tf_op | source)
XLA Modules:
  0.0 226.1 jit_solution(12899465995438801114)
XLA Ops:
  0.0 1.4 copy.6.pot
  1.4 222.9 %shard_map.46 = bf16[768,256]{1,0:T(8,128)(2,1)} custom-call(bf16[768,256]{1,0:T(8,128)(2,1)} %bitcast.3, f32[96,64]{1,0:T(8,128)} %copy.6.pot, bf16[1024,256]{1,0:T(8,128)(2,1)} %r1.1, bf16[1024,256]{1,0:T(8,128)(2,1)} %r2.1), custom_call_target="tpu_custom_call" | custom-call | tf_op jit(solution)/shard_map/pallas_call | solution.py:411
  224.3 1.8 copy.8

commit v2 on v1

--- a/solution.py
+++ b/solution.py
@@ -31,6 +31,8 @@
 PAIR = 2 * OWN
 EXT = PAIR + 12
 CELLS = GRID_X * NY
+PIECES = 2
+PROWS = 1024 // PIECES
 
 
 def aligned(value, multiple):
@@ -39,7 +41,7 @@
 
 def kernel(
     orb, pot, r1, r2, out,
-    oext, dext, vpad, volt, filt, g1, g2, rb1, rb2, pbuf, prec, tq, sq,
+    oext, dext, vpad, potf, volt, filt, g1, g2, rb1, rb2, pbuf, prec, tq, sq,
     swap_s, swap_r, back_s, back_r, loc, halo_s, halo_r,
     g_s, g_r, p_s, p_r, sq_s, sq_r, rz_s, rz_r, ry_s, ry_r,
 ):
@@ -92,57 +94,77 @@
     keep = pltpu.make_async_copy(orb.at[:, pl.ds(mine, HALF)], oext.at[pl.ds(own_at, ROWS)], loc.at[0])
     keep.start()
 
-    def coef_z(i, r, rb):
-        rows = pl.ds(aligned(y * 1024, 1024), 1024)
-        here = rb.at[za, rows]
-        other = remote(r, here, rz_s.at[i, 0], rz_r.at[i, za], device(zh_=1 - zh, za_=zh))
-        near = remote(r, here, rz_s.at[i, 1], rz_r.at[i, za], device(za_=zh))
-        own = pltpu.make_async_copy(r, here, rz_r.at[i, za])
+    def piece(q):
+        return pl.ds(q * PROWS, PROWS)
+
+    def slot_rows(step, q, first=0, count=PROWS):
+        return pl.ds(aligned(around(y, step) * 1024 + q * PROWS + first, 128), count)
+
+    def coef_z(i, r, rb, q):
+        here = rb.at[za, slot_rows(0, q)]
+        other = remote(r.at[piece(q)], here, rz_s.at[i, q, 0], rz_r.at[i, q, za], device(zh_=1 - zh, za_=zh))
+        near = remote(r.at[piece(q)], here, rz_s.at[i, q, 1], rz_r.at[i, q, za], device(za_=zh))
+        own = pltpu.make_async_copy(r.at[piece(q)], here, rz_r.at[i, q, za])
         return other, near, own
 
     def coef_z_start(i, r, rb):
-        other, near, own = coef_z(i, r, rb)
-        other.start()
-
-        @pl.when(za != zh)
-        def _():
-            near.start()
-
-        @pl.when(za == zh)
-        def _():
-            own.start()
-
-    def coef_y(i, rb, part):
-        rows = pl.ds(aligned(y * 1024, 1024), 1024)
+        for q in range(PIECES):
+            other, near, own = coef_z(i, r, rb, q)
+            other.start()
+
+            @pl.when(za != zh)
+            def _():
+                near.start()
+
+            @pl.when(za == zh)
+            def _():
+                own.start()
+
+    def ring(i, rb, part, q, n, step, to, first=0, count=PROWS):
+        rows = slot_rows(step, q, first, count)
+        return remote(
+            rb.at[part, rows], rb.at[part, rows], ry_s.at[i, part, q, n], ry_r.at[i, part, q, n],
+            device(y_=around(y, to)),
+        )
+
+    def coef_near(i, rb, q):
+        return [ring(i, rb, part, q, n, 0, to) for part in range(2) for n, to in ((0, 1), (1, 3))]
+
+    def coef_far(i, rb, q):
+        half = PROWS // 2
         return [
-            remote(
-                rb.at[part, rows], rb.at[part, rows], ry_s.at[i, part, step - 1], ry_r.at[i, part, step - 1],
-                device(y_=around(y, step)),
-            )
-            for step in (1, 3, 2)
+            ring(i, rb, part, q, n, step, to, first, half)
+            for part in range(2)
+            for n, step, to, first in ((2, 3, 1, 0), (3, 1, 3, half))
         ]
 
-    def coef_y_start(i, r, rb):
+    def coef_near_start(i, r, rb, q):
         for part in range(2):
-            pltpu.make_async_copy(r, rb.at[part, pl.ds(aligned(y * 1024, 1024), 1024)], rz_r.at[i, part]).wait()
-            for copy in coef_y(i, rb, part):
-                copy.start()
+            pltpu.make_async_copy(r.at[piece(q)], rb.at[part, slot_rows(0, q)], rz_r.at[i, q, part]).wait()
+        for copy in coef_near(i, rb, q):
+            copy.start()
+
+    def coef_far_start(i, rb, q):
+        for copy in coef_near(i, rb, q):
+            copy.wait_recv()
+        for copy in coef_far(i, rb, q):
+            copy.start()
 
     def coef_wait(i, rb):
-        for part in range(2):
-            for copy in coef_y(i, rb, part):
+        for q in range(PIECES):
+            for copy in coef_far(i, rb, q):
                 copy.wait_recv()
 
     def coef_end(i, r, rb):
-        other, near, own = coef_z(i, r, rb)
-        other.wait_send()
-
-        @pl.when(za != zh)
-        def _():
-            near.wait_send()
-
-        for part in range(2):
-            for copy in coef_y(i, rb, part):
+        for q in range(PIECES):
+            other, near, own = coef_z(i, r, rb, q)
+            other.wait_send()
+
+            @pl.when(za != zh)
+            def _():
+                near.wait_send()
+
+            for copy in coef_near(i, rb, q) + coef_far(i, rb, q):
                 copy.wait_send()
 
     coef_z_start(0, r1, rb1)
@@ -150,8 +172,10 @@
     diagonal = lax.broadcasted_iota(jnp.int32, (NY, NY), 0) == lax.broadcasted_iota(jnp.int32, (NY, NY), 1)
     ones = jnp.ones((NY, HALF), jnp.bfloat16)
 
+    potf[...] = pot[...].astype(jnp.float32)
+
     def spread(i, carry):
-        row = pot[pl.ds(y * PAIR + i, 1), :]
+        row = potf[pl.ds(y * PAIR + i, 1), :]
         square = jnp.where(diagonal, jnp.broadcast_to(row, (NY, NY)), 0.0).astype(jnp.bfloat16)
         volt[i] = jnp.dot(square, ones, preferred_element_type=jnp.float32)
         return carry
@@ -200,6 +224,7 @@
     def field(i, ext):
         for copy in rims(i, ext):
             copy.start()
+        coef_near_start(0, r1, rb1, i)
         widen(ext, 6, PAIR, None)
         for copy in rims(i, ext):
             copy.wait_recv()
@@ -257,22 +282,31 @@
     def send(i, g, slot, j, n, to):
         return remote(block(g, slot, j), block(g, slot, j), g_s.at[i, j, n], g_r.at[i, j, slot], to)
 
+    right, left = device(x_=around(x, 1)), device(x_=around(x, 3))
+
+    def slot_at(step, b):
+        return (around(x, step) * 2 + b) * 2 + core
+
     def own_sends(i, g, j):
-        places = [device(zb_=1 - zb), device(x_=around(x, 1)), device(x_=around(x, 3)), device(x_=around(x, 2)), other_core]
-        return [send(i, g, own_slot, j, n, to) for n, to in enumerate(places)]
+        return [send(i, g, own_slot, j, n, to) for n, to in enumerate((device(zb_=1 - zb), right, left, other_core))]
 
     def pair_sends(i, g, j):
-        slot = (x * 2 + 1 - zb) * 2 + core
-        places = [device(x_=around(x, 1)), device(x_=around(x, 3)), device(x_=around(x, 2)), other_core]
-        return [send(i, g, slot, j, 5 + n, to) for n, to in enumerate(places)]
+        return [send(i, g, slot_at(0, 1 - zb), j, 4 + n, to) for n, to in enumerate((right, left, other_core))]
+
+    def near_sends(i, g, j):
+        sends = []
+        for step, first, to in ((3, 0, right), (1, CROWS // 2, left)):
+            for b in (0, 1):
+                slot = slot_at(step, b)
+                rows = pl.ds(aligned(j * CROWS + first, CROWS // 2), CROWS // 2)
+                part = g.at[slot, rows]
+                n = 7 + len(sends)
+                sends.append(remote(part, part, g_s.at[i, j, n], g_r.at[i, j, slot], to))
+                sends.append(send(i, g, slot, j, n + 1, other_core))
+        return sends
 
     def far_sends(i, g, j):
-        sends = []
-        for step in (1, 3, 2):
-            for b in (0, 1):
-                slot = (around(x, step) * 2 + b) * 2 + core
-                sends.append(send(i, g, slot, j, 9 + len(sends), other_core))
-        return sends
+        return [send(i, g, slot_at(2, b), j, 15 + b, other_core) for b in (0, 1)]
 
     def arrived(i, g, slot, j):
         send(i, g, slot, j, 0, other_core).wait_recv()
@@ -282,20 +316,28 @@
             copy.start()
 
     def gather_pair(i, g, j):
-        arrived(i, g, (x * 2 + 1 - zb) * 2 + core, j)
+        arrived(i, g, slot_at(0, 1 - zb), j)
         for copy in pair_sends(i, g, j):
             copy.start()
 
+    def gather_near(i, g, j):
+        for step in (3, 1):
+            for b in (0, 1):
+                arrived(i, g, slot_at(step, b), j)
+        for copy in near_sends(i, g, j):
+            copy.start()
+
     def gather_far(i, g, j):
+        for b in (0, 1):
+            arrived(i, g, slot_at(2, b), j)
         for copy in far_sends(i, g, j):
-            copy.wait_recv()
             copy.start()
         for slot in range(8):
             arrived(i, g, slot * 2 + 1 - core, j)
 
     def gather_end(i, g):
         def step(j, carry):
-            for copy in own_sends(i, g, j) + pair_sends(i, g, j) + far_sends(i, g, j):
+            for copy in own_sends(i, g, j) + pair_sends(i, g, j) + near_sends(i, g, j) + far_sends(i, g, j):
                 copy.wait_send()
             return carry
 
@@ -314,27 +356,30 @@
     def partial_send(i, j):
         return remote(pbuf.at[i, j], prec.at[i, j], p_s.at[i, j], p_r.at[i, j], device(za_=1 - za))
 
-    def rotate(i, g, rb):
-        def step(j, carry):
-            gather_far(i, g, j)
-            pbuf[i, j] = product(g, rb, j, 1 - za).astype(jnp.bfloat16)
-            partial_send(i, j).start()
-            tq[j] = product(g, rb, j, za)
-            return carry
-
-        lax.fori_loop(0, CHUNKS, step, 0)
-
-    coef_y_start(0, r1, rb1)
-    coef_z_start(1, r2, rb2)
+    def multiply(i, g, rb, j):
+        gather_far(i, g, j)
+        pbuf[i, j] = product(g, rb, j, 1 - za).astype(jnp.bfloat16)
+        partial_send(i, j).start()
+        tq[j] = product(g, rb, j, za)
+
+    coef_far_start(0, rb1, 0)
     for j in range(CHUNKS):
         stay(j).wait()
         back(j).wait_recv()
         gather_own(0, g1, j)
+    coef_far_start(0, rb1, 1)
     for j in range(CHUNKS):
         gather_pair(0, g1, j)
+    coef_z_start(1, r2, rb2)
+    gather_near(0, g1, 0)
+    gather_near(0, g1, 1)
     coef_wait(0, rb1)
-    rotate(0, g1, rb1)
-    coef_y_start(1, r2, rb2)
+    multiply(0, g1, rb1, 0)
+    gather_near(0, g1, 2)
+    multiply(0, g1, rb1, 1)
+    coef_near_start(1, r2, rb2, 0)
+    multiply(0, g1, rb1, 2)
+    coef_near_start(1, r2, rb2, 1)
 
     sums = jnp.zeros((8, LANES), jnp.float32)
     for j in range(CHUNKS):
@@ -372,10 +417,17 @@
         lax.fori_loop(0, CROWS // 32, normalize, 0)
         gather_own(1, g2, j)
 
+    coef_far_start(1, rb2, 0)
     for j in range(CHUNKS):
         gather_pair(1, g2, j)
+    coef_far_start(1, rb2, 1)
+    gather_near(1, g2, 0)
+    gather_near(1, g2, 1)
     coef_wait(1, rb2)
-    rotate(1, g2, rb2)
+    multiply(1, g2, rb2, 0)
+    gather_near(1, g2, 2)
+    multiply(1, g2, rb2, 1)
+    multiply(1, g2, rb2, 2)
 
     for j in range(CHUNKS):
         partial_send(1, j).wait_recv()
@@ -417,6 +469,7 @@
             pltpu.VMEM((EXT * NY, HALF), bf16),
             pltpu.VMEM((EXT * NY, HALF), bf16),
             pltpu.VMEM((EXT, NY + 16, HALF), f32),
+            pltpu.VMEM((GRID_X, NY), f32),
             pltpu.VMEM((PAIR, NY, HALF), f32),
             pltpu.VMEM((PAIR * NY, HALF), bf16),
             pltpu.VMEM((16, ROWS, LANES), bf16),
@@ -431,16 +484,16 @@
             dma((CHUNKS,)), dma((CHUNKS,)),
             dma((1 + CHUNKS,)),
             dma((2, 2)), dma((2, 2)),
-            dma((2, CHUNKS, 15)), dma((2, CHUNKS, 16)),
+            dma((2, CHUNKS, 17)), dma((2, CHUNKS, 16)),
             dma((2, CHUNKS)), dma((2, CHUNKS)),
             dma((7,)), dma((7,)),
-            dma((2, 2)), dma((2, 2)),
-            dma((2, 2, 3)), dma((2, 2, 3)),
+            dma((2, PIECES, 2)), dma((2, PIECES, 2)),
+            dma((2, 2, PIECES, 4)), dma((2, 2, PIECES, 4)),
         ],
         compiler_params=pltpu.CompilerParams(
             collective_id=0, has_side_effects=True, vmem_limit_bytes=56 << 20
         ),
-    )(orbitals.reshape(ROWS, LANES), potential.astype(f32), rot_first, rot_second)
+    )(orbitals.reshape(ROWS, LANES), potential, rot_first, rot_second)
     return result.reshape(OWN, NY, LANES)
 
 

time: 226 us -> 179 us (0.79)
  Pallas kernels: 223 us -> 175 us
    pallas_call x1, Pallas kernels: 223 us -> 175 us  [shards(): pl.pallas_call(kernel, out_shape=jax.ShapeDtypeStruct((ROWS, LANES), bf16...]
where the time goes in v2:
time: 179 us
  Pallas kernels  175 us (98%)
  local copies, waits for them, and re-layouts  3.18 us (2%)
    pallas_call x1, Pallas kernels, shards(): pl.pallas_call(kernel, out_shape=jax.ShapeDtypeStruct((ROWS, LANES), bf16...  175 us

profile of v2, /device:TPU:1, one launch (start us, length us, event | category | flops | bytes accessed | tf_op | source)
XLA Modules:
  0.0 178.7 jit_solution(16990929692815364615)
XLA Ops:
  0.0 1.4 copy.5.pot
  1.4 175.5 %shard_map.46 = bf16[768,256]{1,0:T(8,128)(2,1)} custom-call(bf16[768,256]{1,0:T(8,128)(2,1)} %bitcast.3, bf16[96,64]{1,0:T(8,128)(2,1)} %copy.5.pot, bf16[1024,256]{1,0:T(8,128)(2,1)} %r1.1, bf16[1024,256]{1,0:T(8,128)(2,1)} %r2.1), custom_call_target="tpu_custom_call" | custom-call | tf_op jit(solution)/shard_map/pallas_call | solution.py:463
  176.9 1.8 copy.7

commit v3 on v2

--- a/solution.py
+++ b/solution.py
@@ -31,7 +31,7 @@
 PAIR = 2 * OWN
 EXT = PAIR + 12
 CELLS = GRID_X * NY
-PIECES = 2
+PIECES = 4
 PROWS = 1024 // PIECES
 
 
@@ -41,9 +41,9 @@
 
 def kernel(
     orb, pot, r1, r2, out,
-    oext, dext, vpad, potf, volt, filt, g1, g2, rb1, rb2, pbuf, prec, tq, sq,
+    oext, dext, vpad, potf, volt, filt, g1, g2, rb1, rb2, relay, pbuf, prec, tq, sq,
     swap_s, swap_r, back_s, back_r, loc, halo_s, halo_r,
-    g_s, g_r, p_s, p_r, sq_s, sq_r, rz_s, rz_r, ry_s, ry_r,
+    g_s, g_r, p_s, p_r, sq_s, sq_r, rz_s, rz_r, rl_r, ry_s, ry_r,
 ):
     band = lax.axis_index("band")
     dom = lax.axis_index("dom")
@@ -104,21 +104,36 @@
         here = rb.at[za, slot_rows(0, q)]
         other = remote(r.at[piece(q)], here, rz_s.at[i, q, 0], rz_r.at[i, q, za], device(zh_=1 - zh, za_=zh))
         near = remote(r.at[piece(q)], here, rz_s.at[i, q, 1], rz_r.at[i, q, za], device(za_=zh))
+        over = remote(
+            r.at[piece(q)], relay.at[i, piece(q)], rz_s.at[i, q, 0], rl_r.at[i, q], device(zh_=1 - zh, za_=1 - za)
+        )
+        onward = remote(
+            relay.at[i, piece(q)], rb.at[1 - za, slot_rows(0, q)], rz_s.at[i, q, 1], rz_r.at[i, q, 1 - za],
+            device(za_=1 - za),
+        )
         own = pltpu.make_async_copy(r.at[piece(q)], here, rz_r.at[i, q, za])
-        return other, near, own
-
-    def coef_z_start(i, r, rb):
-        for q in range(PIECES):
-            other, near, own = coef_z(i, r, rb, q)
+        return other, near, over, onward, own
+
+    def coef_z_start(i, r, rb, q):
+        other, near, over, onward, own = coef_z(i, r, rb, q)
+
+        @pl.when(za != zh)
+        def _():
             other.start()
-
-            @pl.when(za != zh)
-            def _():
-                near.start()
-
-            @pl.when(za == zh)
-            def _():
-                own.start()
+            near.start()
+
+        @pl.when(za == zh)
+        def _():
+            over.start()
+            own.start()
+
+    def coef_onward(i, r, rb, q):
+        other, near, over, onward, own = coef_z(i, r, rb, q)
+
+        @pl.when(za == zh)
+        def _():
+            over.wait_recv()
+            onward.start()
 
     def ring(i, rb, part, q, n, step, to, first=0, count=PROWS):
         rows = slot_rows(step, q, first, count)
@@ -157,17 +172,22 @@
 
     def coef_end(i, r, rb):
         for q in range(PIECES):
-            other, near, own = coef_z(i, r, rb, q)
-            other.wait_send()
+            other, near, over, onward, own = coef_z(i, r, rb, q)
 
             @pl.when(za != zh)
             def _():
+                other.wait_send()
                 near.wait_send()
+
+            @pl.when(za == zh)
+            def _():
+                over.wait_send()
+                onward.wait_send()
 
             for copy in coef_near(i, rb, q) + coef_far(i, rb, q):
                 copy.wait_send()
 
-    coef_z_start(0, r1, rb1)
+    coef_z_start(0, r1, rb1, 0)
 
     diagonal = lax.broadcasted_iota(jnp.int32, (NY, NY), 0) == lax.broadcasted_iota(jnp.int32, (NY, NY), 1)
     ones = jnp.ones((NY, HALF), jnp.bfloat16)
@@ -221,19 +241,21 @@
             )
         return -0.5 * lap + volt[i] * center, center
 
-    def field(i, ext):
-        for copy in rims(i, ext):
-            copy.start()
-        coef_near_start(0, r1, rb1, i)
-        widen(ext, 6, PAIR, None)
-        for copy in rims(i, ext):
-            copy.wait_recv()
-        widen(ext, 0, 6, y > 0)
-        widen(ext, 30, 6, y < 3)
-
+    coef_z_start(0, r1, rb1, 1)
+    coef_onward(0, r1, rb1, 0)
     keep.wait()
     swap.wait_recv()
-    field(0, oext)
+    for copy in rims(0, oext):
+        copy.start()
+    coef_z_start(0, r1, rb1, 2)
+    coef_z_start(0, r1, rb1, 3)
+    coef_near_start(0, r1, rb1, 0)
+    widen(oext, 6, PAIR, None)
+    for copy in rims(0, oext):
+        copy.wait_recv()
+    widen(oext, 0, 6, y > 0)
+    widen(oext, 30, 6, y < 3)
+    coef_onward(0, r1, rb1, 1)
 
     def first(i, carry):
         value, center = applied(i)
@@ -243,7 +265,15 @@
         return carry
 
     lax.fori_loop(0, PAIR, first, 0)
-    field(1, dext)
+    for copy in rims(1, dext):
+        copy.start()
+    coef_near_start(0, r1, rb1, 1)
+    widen(dext, 6, PAIR, None)
+    for copy in rims(1, dext):
+        copy.wait_recv()
+    widen(dext, 0, 6, y > 0)
+    widen(dext, 30, 6, y < 3)
+    coef_onward(0, r1, rb1, 2)
 
     def second(i, carry):
         value, center = applied(i)
@@ -270,6 +300,9 @@
     for j in range(CHUNKS):
         lax.fori_loop((1 - zh) * OWN + j * per, (1 - zh) * OWN + (j + 1) * per, second, 0)
         back(j).start()
+    coef_far_start(0, rb1, 0)
+    coef_near_start(0, r1, rb1, 2)
+    coef_onward(0, r1, rb1, 3)
     for j in range(CHUNKS):
         lax.fori_loop(zh * OWN + j * per, zh * OWN + (j + 1) * per, second, 0)
         stay(j).start()
@@ -362,24 +395,31 @@
         partial_send(i, j).start()
         tq[j] = product(g, rb, j, za)
 
-    coef_far_start(0, rb1, 0)
     for j in range(CHUNKS):
         stay(j).wait()
         back(j).wait_recv()
         gather_own(0, g1, j)
+    coef_near_start(0, r1, rb1, 3)
     coef_far_start(0, rb1, 1)
     for j in range(CHUNKS):
         gather_pair(0, g1, j)
-    coef_z_start(1, r2, rb2)
+    coef_far_start(0, rb1, 2)
+    for q in range(PIECES):
+        coef_z_start(1, r2, rb2, q)
     gather_near(0, g1, 0)
     gather_near(0, g1, 1)
+    coef_far_start(0, rb1, 3)
     coef_wait(0, rb1)
     multiply(0, g1, rb1, 0)
+    coef_onward(1, r2, rb2, 0)
     gather_near(0, g1, 2)
+    coef_onward(1, r2, rb2, 1)
     multiply(0, g1, rb1, 1)
+    coef_onward(1, r2, rb2, 2)
     coef_near_start(1, r2, rb2, 0)
     multiply(0, g1, rb1, 2)
     coef_near_start(1, r2, rb2, 1)
+    coef_onward(1, r2, rb2, 3)
 
     sums = jnp.zeros((8, LANES), jnp.float32)
     for j in range(CHUNKS):
@@ -417,12 +457,16 @@
         lax.fori_loop(0, CROWS // 32, normalize, 0)
         gather_own(1, g2, j)
 
+    coef_near_start(1, r2, rb2, 2)
     coef_far_start(1, rb2, 0)
+    coef_near_start(1, r2, rb2, 3)
+    coef_far_start(1, rb2, 1)
     for j in range(CHUNKS):
         gather_pair(1, g2, j)
-    coef_far_start(1, rb2, 1)
+    coef_far_start(1, rb2, 2)
     gather_near(1, g2, 0)
     gather_near(1, g2, 1)
+    coef_far_start(1, rb2, 3)
     coef_wait(1, rb2)
     multiply(1, g2, rb2, 0)
     gather_near(1, g2, 2)
@@ -476,6 +520,7 @@
             pltpu.VMEM((16, ROWS, LANES), bf16),
             pltpu.VMEM((2, 4096, LANES), bf16),
             pltpu.VMEM((2, 4096, LANES), bf16),
+            pltpu.VMEM((2, 1024, LANES), bf16),
             pltpu.VMEM((2, CHUNKS, CROWS, LANES), bf16),
             pltpu.VMEM((2, CHUNKS, CROWS, LANES), bf16),
             pltpu.VMEM((CHUNKS, CROWS, LANES), f32),
@@ -487,7 +532,7 @@
             dma((2, CHUNKS, 17)), dma((2, CHUNKS, 16)),
             dma((2, CHUNKS)), dma((2, CHUNKS)),
             dma((7,)), dma((7,)),
-            dma((2, PIECES, 2)), dma((2, PIECES, 2)),
+            dma((2, PIECES, 2)), dma((2, PIECES, 2)), dma((2, PIECES)),
             dma((2, 2, PIECES, 4)), dma((2, 2, PIECES, 4)),
         ],
         compiler_params=pltpu.CompilerParams(

time: 179 us -> 179 us (level)
  no operation moved by 1% of the time
where the time goes in v3:
time: 179 us; the launch traced here: 177 us
  Pallas kernels  174 us (97%)
  local copies, waits for them, and re-layouts  3.18 us (2%)
    pallas_call x1, Pallas kernels, shards(): pl.pallas_call(kernel, out_shape=jax.ShapeDtypeStruct((ROWS, LANES), bf16...  174 us

profile of v3, /device:TPU:1, one launch (start us, length us, event | category | flops | bytes accessed | tf_op | source)
XLA Modules:
  0.0 177.0 jit_solution(14857242767318582831)
XLA Ops:
  0.0 1.4 copy.5.pot
  1.4 173.8 %shard_map.46 = bf16[768,256]{1,0:T(8,128)(2,1)} custom-call(bf16[768,256]{1,0:T(8,128)(2,1)} %bitcast.3, bf16[96,64]{1,0:T(8,128)(2,1)} %copy.5.pot, bf16[1024,256]{1,0:T(8,128)(2,1)} %r1.1, bf16[1024,256]{1,0:T(8,128)(2,1)} %r2.1), custom_call_target="tpu_custom_call" | custom-call | tf_op jit(solution)/shard_map/pallas_call | solution.py:507
  175.2 1.8 copy.7

commit v4 on v3

--- a/solution.py
+++ b/solution.py
@@ -31,8 +31,25 @@
 PAIR = 2 * OWN
 EXT = PAIR + 12
 CELLS = GRID_X * NY
-PIECES = 4
+PIECES = 2
 PROWS = 1024 // PIECES
+
+
+SCHEDULE = {
+    "swap": "z00",
+    "rim0": "z01",
+    "first": "o00",
+    "back": "o01",
+    "stay": "n00",
+    "own00": "n01",
+    "own02": "z10 f00",
+    "pair00": "z11",
+    "near00": "f01",
+    "near01": "o10 o11",
+    "mul00": "n10 n11",
+    "turn2": "f10",
+    "norm": "f11",
+}
 
 
 def aligned(value, multiple):
@@ -41,9 +58,9 @@
 
 def kernel(
     orb, pot, r1, r2, out,
-    oext, dext, vpad, potf, volt, filt, g1, g2, rb1, rb2, relay, pbuf, prec, tq, sq,
+    oext, dext, vpad, potf, volt, filt, g1, g2, rb1, rb2, relay, pbuf, prec, tq, sq, norm, lhs,
     swap_s, swap_r, back_s, back_r, loc, halo_s, halo_r,
-    g_s, g_r, p_s, p_r, sq_s, sq_r, rz_s, rz_r, rl_r, ry_s, ry_r,
+    g_s, g_r, p_s, p_r, sq_s, sq_r, n_s, n_r, rz_s, rz_r, rl_r, ry_s, ry_r,
 ):
     band = lax.axis_index("band")
     dom = lax.axis_index("dom")
@@ -78,6 +95,7 @@
         partners.append(device(x_=around(x, step)))
         partners.append(device(y_=around(y, step)))
         partners.append(device(y_=around(y, step), zh_=1 - zh))
+        partners.append(device(x_=around(x, step), zb_=1 - zb))
     partners.append(device(core_=1 - core))
     for to in partners:
         pl.semaphore_signal(barrier, inc=1, device_id=to, device_id_type=MESH)
@@ -187,7 +205,23 @@
             for copy in coef_near(i, rb, q) + coef_far(i, rb, q):
                 copy.wait_send()
 
-    coef_z_start(0, r1, rb1, 0)
+
+    rotations = ((r1, rb1), (r2, rb2))
+
+    def at(point):
+        for word in SCHEDULE.get(point, "").split():
+            i, q = int(word[1]), int(word[2])
+            r, rb = rotations[i]
+            if word[0] == "z":
+                coef_z_start(i, r, rb, q)
+            elif word[0] == "o":
+                coef_onward(i, r, rb, q)
+            elif word[0] == "n":
+                coef_near_start(i, r, rb, q)
+            else:
+                coef_far_start(i, rb, q)
+
+    at("start")
 
     diagonal = lax.broadcasted_iota(jnp.int32, (NY, NY), 0) == lax.broadcasted_iota(jnp.int32, (NY, NY), 1)
     ones = jnp.ones((NY, HALF), jnp.bfloat16)
@@ -241,21 +275,18 @@
             )
         return -0.5 * lap + volt[i] * center, center
 
-    coef_z_start(0, r1, rb1, 1)
-    coef_onward(0, r1, rb1, 0)
+    at("volt")
     keep.wait()
     swap.wait_recv()
     for copy in rims(0, oext):
         copy.start()
-    coef_z_start(0, r1, rb1, 2)
-    coef_z_start(0, r1, rb1, 3)
-    coef_near_start(0, r1, rb1, 0)
+    at("swap")
     widen(oext, 6, PAIR, None)
     for copy in rims(0, oext):
         copy.wait_recv()
     widen(oext, 0, 6, y > 0)
     widen(oext, 30, 6, y < 3)
-    coef_onward(0, r1, rb1, 1)
+    at("rim0")
 
     def first(i, carry):
         value, center = applied(i)
@@ -267,13 +298,13 @@
     lax.fori_loop(0, PAIR, first, 0)
     for copy in rims(1, dext):
         copy.start()
-    coef_near_start(0, r1, rb1, 1)
+    at("first")
     widen(dext, 6, PAIR, None)
     for copy in rims(1, dext):
         copy.wait_recv()
     widen(dext, 0, 6, y > 0)
     widen(dext, 30, 6, y < 3)
-    coef_onward(0, r1, rb1, 2)
+    at("rim1")
 
     def second(i, carry):
         value, center = applied(i)
@@ -300,9 +331,7 @@
     for j in range(CHUNKS):
         lax.fori_loop((1 - zh) * OWN + j * per, (1 - zh) * OWN + (j + 1) * per, second, 0)
         back(j).start()
-    coef_far_start(0, rb1, 0)
-    coef_near_start(0, r1, rb1, 2)
-    coef_onward(0, r1, rb1, 3)
+    at("back")
     for j in range(CHUNKS):
         lax.fori_loop(zh * OWN + j * per, zh * OWN + (j + 1) * per, second, 0)
         stay(j).start()
@@ -395,43 +424,50 @@
         partial_send(i, j).start()
         tq[j] = product(g, rb, j, za)
 
+    at("stay")
     for j in range(CHUNKS):
         stay(j).wait()
         back(j).wait_recv()
         gather_own(0, g1, j)
-    coef_near_start(0, r1, rb1, 3)
-    coef_far_start(0, rb1, 1)
+        at(f"own0{j}")
     for j in range(CHUNKS):
         gather_pair(0, g1, j)
-    coef_far_start(0, rb1, 2)
-    for q in range(PIECES):
-        coef_z_start(1, r2, rb2, q)
+        at(f"pair0{j}")
     gather_near(0, g1, 0)
+    at("near00")
     gather_near(0, g1, 1)
-    coef_far_start(0, rb1, 3)
+    at("near01")
     coef_wait(0, rb1)
     multiply(0, g1, rb1, 0)
-    coef_onward(1, r2, rb2, 0)
+    at("mul00")
     gather_near(0, g1, 2)
-    coef_onward(1, r2, rb2, 1)
+    at("near02")
     multiply(0, g1, rb1, 1)
-    coef_onward(1, r2, rb2, 2)
-    coef_near_start(1, r2, rb2, 0)
-    multiply(0, g1, rb1, 2)
-    coef_near_start(1, r2, rb2, 1)
-    coef_onward(1, r2, rb2, 3)
-
-    sums = jnp.zeros((8, LANES), jnp.float32)
-    for j in range(CHUNKS):
+    at("mul01")
+
+    def turned(j, sums):
         partial_send(0, j).wait_recv()
 
-        def squares(n, total):
+        def step(n, total):
             rows = pl.ds(aligned(n * 32, 32), 32)
             value = tq[j, rows, :] + prec[0, j, rows, :].astype(jnp.float32)
-            tq[j, rows, :] = value
+            g2[own_slot, pl.ds(aligned(j * CROWS + n * 32, 32), 32), :] = value.astype(jnp.bfloat16)
             return total + jnp.sum((value * value).reshape(4, 8, LANES), axis=0)
 
-        sums = lax.fori_loop(0, CROWS // 32, squares, sums)
+        sums = lax.fori_loop(0, CROWS // 32, step, sums)
+        gather_own(1, g2, j)
+        return sums
+
+    sums = turned(0, jnp.zeros((8, LANES), jnp.float32))
+    at("turn0")
+    multiply(0, g1, rb1, 2)
+    at("mul02")
+    sums = turned(1, sums)
+    at("turn1")
+    gather_pair(1, g2, 0)
+    at("pair10")
+    sums = turned(2, sums)
+    at("turn2")
     sq[dom] = sums
 
     def share(step):
@@ -446,34 +482,59 @@
     for d in range(1, 8):
         total = total + sq[d]
     mean_square = jnp.sum(total, axis=0, keepdims=True) * (1.0 / CELLS)
-    scale = 1.0 / jnp.sqrt(mean_square + 1e-06)
-    for j in range(CHUNKS):
-
-        def normalize(n, carry):
-            rows = pl.ds(aligned(n * 32, 32), 32)
-            g2[own_slot, pl.ds(aligned(j * CROWS + n * 32, 32), 32), :] = (tq[j, rows, :] * scale).astype(jnp.bfloat16)
+    norm[own_slot] = jnp.broadcast_to(1.0 / jnp.sqrt(mean_square + 1e-06), (8, LANES))
+
+    def norm_send(slot, n, to):
+        return remote(norm.at[slot], norm.at[slot], n_s.at[n], n_r.at[slot], to)
+
+    others = [(step, b) for step in range(4) for b in (0, 1) if step or b]
+
+    def norm_sends():
+        sends = [norm_send(own_slot, 0, other_core)]
+        for n, (step, b) in enumerate(others):
+            sends.append(norm_send(own_slot, 1 + n, device(x_=around(x, step), zb_=(zb + b) % 2)))
+        return sends
+
+    def norm_forwards():
+        return [
+            norm_send(slot_at(step, (zb + b) % 2), 8 + n, other_core) for n, (step, b) in enumerate(others)
+        ]
+
+    for copy in norm_sends():
+        copy.start()
+    at("norm")
+    gather_pair(1, g2, 1)
+    at("pair11")
+    gather_near(1, g2, 0)
+    at("near10")
+    gather_pair(1, g2, 2)
+    at("pair12")
+    for copy in norm_forwards():
+        copy.wait_recv()
+        copy.start()
+    gather_near(1, g2, 1)
+    at("near11")
+    for slot in range(8):
+        norm_send(slot * 2 + 1 - core, 0, other_core).wait_recv()
+
+    def normalize(j):
+        def step(slot, carry):
+            for n in range(CROWS // 64):
+                rows = pl.ds(aligned(j * CROWS + n * 64, 64), 64)
+                value = g2[slot, rows, :].astype(jnp.float32) * norm[slot, 0:1, :]
+                lhs[slot, n * 64 : (n + 1) * 64, :] = value.astype(jnp.bfloat16)
             return carry
 
-        lax.fori_loop(0, CROWS // 32, normalize, 0)
-        gather_own(1, g2, j)
-
-    coef_near_start(1, r2, rb2, 2)
-    coef_far_start(1, rb2, 0)
-    coef_near_start(1, r2, rb2, 3)
-    coef_far_start(1, rb2, 1)
-    for j in range(CHUNKS):
-        gather_pair(1, g2, j)
-    coef_far_start(1, rb2, 2)
-    gather_near(1, g2, 0)
-    gather_near(1, g2, 1)
-    coef_far_start(1, rb2, 3)
-    coef_wait(1, rb2)
-    multiply(1, g2, rb2, 0)
-    gather_near(1, g2, 2)
-    multiply(1, g2, rb2, 1)
-    multiply(1, g2, rb2, 2)
-
-    for j in range(CHUNKS):
+        lax.fori_loop(0, 16, step, 0)
+
+    def multiply_normed(j):
+        gather_far(1, g2, j)
+        normalize(j)
+        pbuf[1, j] = product(lhs, rb2, 0, 1 - za).astype(jnp.bfloat16)
+        partial_send(1, j).start()
+        tq[j] = product(lhs, rb2, 0, za)
+
+    def finished(j):
         partial_send(1, j).wait_recv()
 
         def finish(n, carry):
@@ -484,6 +545,15 @@
             return carry
 
         lax.fori_loop(0, CROWS // 32, finish, 0)
+
+    coef_wait(1, rb2)
+    multiply_normed(0)
+    gather_near(1, g2, 2)
+    multiply_normed(1)
+    finished(0)
+    multiply_normed(2)
+    finished(1)
+    finished(2)
 
     swap.wait_send()
     for j in range(CHUNKS):
@@ -498,6 +568,8 @@
             partial_send(i, j).wait_send()
     for step in range(1, 8):
         share(step).wait_send()
+    for copy in norm_sends() + norm_forwards():
+        copy.wait_send()
 
 
 def shards(orbitals, potential, rot_first, rot_second):
@@ -525,6 +597,8 @@
             pltpu.VMEM((2, CHUNKS, CROWS, LANES), bf16),
             pltpu.VMEM((CHUNKS, CROWS, LANES), f32),
             pltpu.VMEM((8, 8, LANES), f32),
+            pltpu.VMEM((16, 8, LANES), f32),
+            pltpu.VMEM((16, CROWS, LANES), bf16),
             dma, dma,
             dma((CHUNKS,)), dma((CHUNKS,)),
             dma((1 + CHUNKS,)),
@@ -532,6 +606,7 @@
             dma((2, CHUNKS, 17)), dma((2, CHUNKS, 16)),
             dma((2, CHUNKS)), dma((2, CHUNKS)),
             dma((7,)), dma((7,)),
+            dma((15,)), dma((16,)),
             dma((2, PIECES, 2)), dma((2, PIECES, 2)), dma((2, PIECES)),
             dma((2, 2, PIECES, 4)), dma((2, 2, PIECES, 4)),
         ],

time: 179 us -> 177 us (0.989); the launches traced: 177 us -> 177 us
  no operation moved by 1% of the time
where the time goes in v4:
time: 177 us
  Pallas kernels  174 us (98%)
  local copies, waits for them, and re-layouts  3.18 us (2%)
    pallas_call x1, Pallas kernels, shards(): pl.pallas_call(kernel, out_shape=jax.ShapeDtypeStruct((ROWS, LANES), bf16...  174 us

profile of v4, /device:TPU:1, one launch (start us, length us, event | category | flops | bytes accessed | tf_op | source)
XLA Modules:
  0.0 176.8 jit_solution(10686108448847881882)
XLA Ops:
  0.0 1.4 copy.5.pot
  1.4 173.6 %shard_map.46 = bf16[768,256]{1,0:T(8,128)(2,1)} custom-call(bf16[768,256]{1,0:T(8,128)(2,1)} %bitcast.3, bf16[96,64]{1,0:T(8,128)(2,1)} %copy.5.pot, bf16[1024,256]{1,0:T(8,128)(2,1)} %r1.1, bf16[1024,256]{1,0:T(8,128)(2,1)} %r2.1), custom_call_target="tpu_custom_call" | custom-call | tf_op jit(solution)/shard_map/pallas_call | solution.py:579
  175.0 1.8 copy.7

commit v5 on v4

--- a/solution.py
+++ b/solution.py
@@ -32,23 +32,18 @@
 EXT = PAIR + 12
 CELLS = GRID_X * NY
 PIECES = 2
-PROWS = 1024 // PIECES
 
 
 SCHEDULE = {
-    "swap": "z00",
-    "rim0": "z01",
-    "first": "o00",
-    "back": "o01",
-    "stay": "n00",
-    "own00": "n01",
-    "own02": "z10 f00",
-    "pair00": "z11",
-    "near00": "f01",
-    "near01": "o10 o11",
-    "mul00": "n10 n11",
-    "turn2": "f10",
-    "norm": "f11",
+    "start": "z00",
+    "swap": "z01",
+    "rim0": "n00",
+    "back": "n01",
+    "stay": "z10",
+    "own02": "f00 f01",
+    "pair02": "z11 n10",
+    "mul00": "n11",
+    "turn2": "f10 f11",
 }
 
 
@@ -58,9 +53,9 @@
 
 def kernel(
     orb, pot, r1, r2, out,
-    oext, dext, vpad, potf, volt, filt, g1, g2, rb1, rb2, relay, pbuf, prec, tq, sq, norm, lhs,
+    oext, dext, vpad, potf, volt, filt, g1, g2, rb1, rb2, pbuf, prec, tq, sq, norm, lhs,
     swap_s, swap_r, back_s, back_r, loc, halo_s, halo_r,
-    g_s, g_r, p_s, p_r, sq_s, sq_r, n_s, n_r, rz_s, rz_r, rl_r, ry_s, ry_r,
+    g_s, g_r, p_s, p_r, sq_s, sq_r, n_s, n_r, rz_s, rz_r, ry_s, ry_r,
 ):
     band = lax.axis_index("band")
     dom = lax.axis_index("dom")
@@ -95,7 +90,7 @@
         partners.append(device(x_=around(x, step)))
         partners.append(device(y_=around(y, step)))
         partners.append(device(y_=around(y, step), zh_=1 - zh))
-        partners.append(device(x_=around(x, step), zb_=1 - zb))
+        partners.append(device(x_=around(x, step), za_=1 - za))
     partners.append(device(core_=1 - core))
     for to in partners:
         pl.semaphore_signal(barrier, inc=1, device_id=to, device_id_type=MESH)
@@ -112,49 +107,26 @@
     keep = pltpu.make_async_copy(orb.at[:, pl.ds(mine, HALF)], oext.at[pl.ds(own_at, ROWS)], loc.at[0])
     keep.start()
 
-    def piece(q):
-        return pl.ds(q * PROWS, PROWS)
-
-    def slot_rows(step, q, first=0, count=PROWS):
-        return pl.ds(aligned(around(y, step) * 1024 + q * PROWS + first, 128), count)
-
     def coef_z(i, r, rb, q):
-        here = rb.at[za, slot_rows(0, q)]
-        other = remote(r.at[piece(q)], here, rz_s.at[i, q, 0], rz_r.at[i, q, za], device(zh_=1 - zh, za_=zh))
-        near = remote(r.at[piece(q)], here, rz_s.at[i, q, 1], rz_r.at[i, q, za], device(za_=zh))
-        over = remote(
-            r.at[piece(q)], relay.at[i, piece(q)], rz_s.at[i, q, 0], rl_r.at[i, q], device(zh_=1 - zh, za_=1 - za)
-        )
-        onward = remote(
-            relay.at[i, piece(q)], rb.at[1 - za, slot_rows(0, q)], rz_s.at[i, q, 1], rz_r.at[i, q, 1 - za],
-            device(za_=1 - za),
-        )
-        own = pltpu.make_async_copy(r.at[piece(q)], here, rz_r.at[i, q, za])
-        return other, near, over, onward, own
+        copies = []
+        for n, (other_half, other_zb) in enumerate(((0, 0), (0, 1), (1, 0), (1, 1))):
+            to_zb = (zb + other_zb) % 2
+            source = r.at[pl.ds(aligned(to_zb * 512 + q * 256, 256), 256)]
+            place = rb.at[zb, pl.ds(aligned(((y * 2 + q) * 2 + zh) * 256, 256), 256)]
+            arrival = rz_r.at[i, q, zh * 2 + zb]
+            if n == 0:
+                copies.append(pltpu.make_async_copy(source, place, arrival))
+            else:
+                to = device(zh_=(zh + other_half) % 2, zb_=to_zb)
+                copies.append(remote(source, place, rz_s.at[i, q, n - 1], arrival, to))
+        return copies
 
     def coef_z_start(i, r, rb, q):
-        other, near, over, onward, own = coef_z(i, r, rb, q)
-
-        @pl.when(za != zh)
-        def _():
-            other.start()
-            near.start()
-
-        @pl.when(za == zh)
-        def _():
-            over.start()
-            own.start()
-
-    def coef_onward(i, r, rb, q):
-        other, near, over, onward, own = coef_z(i, r, rb, q)
-
-        @pl.when(za == zh)
-        def _():
-            over.wait_recv()
-            onward.start()
-
-    def ring(i, rb, part, q, n, step, to, first=0, count=PROWS):
-        rows = slot_rows(step, q, first, count)
+        for copy in coef_z(i, r, rb, q):
+            copy.start()
+
+    def ring(i, rb, part, q, n, step, to, first=0, count=512):
+        rows = pl.ds(aligned((around(y, step) * 2 + q) * 512 + first, 256), count)
         return remote(
             rb.at[part, rows], rb.at[part, rows], ry_s.at[i, part, q, n], ry_r.at[i, part, q, n],
             device(y_=around(y, to)),
@@ -164,16 +136,17 @@
         return [ring(i, rb, part, q, n, 0, to) for part in range(2) for n, to in ((0, 1), (1, 3))]
 
     def coef_far(i, rb, q):
-        half = PROWS // 2
         return [
-            ring(i, rb, part, q, n, step, to, first, half)
+            ring(i, rb, part, q, n, step, to, first, 256)
             for part in range(2)
-            for n, step, to, first in ((2, 3, 1, 0), (3, 1, 3, half))
+            for n, step, to, first in ((2, 3, 1, 0), (3, 1, 3, 256))
         ]
 
     def coef_near_start(i, r, rb, q):
-        for part in range(2):
-            pltpu.make_async_copy(r.at[piece(q)], rb.at[part, slot_rows(0, q)], rz_r.at[i, q, part]).wait()
+        for half in range(2):
+            for part in range(2):
+                place = rb.at[part, pl.ds(aligned(((y * 2 + q) * 2 + half) * 256, 256), 256)]
+                pltpu.make_async_copy(r.at[pl.ds(0, 256)], place, rz_r.at[i, q, half * 2 + part]).wait()
         for copy in coef_near(i, rb, q):
             copy.start()
 
@@ -190,21 +163,8 @@
 
     def coef_end(i, r, rb):
         for q in range(PIECES):
-            other, near, over, onward, own = coef_z(i, r, rb, q)
-
-            @pl.when(za != zh)
-            def _():
-                other.wait_send()
-                near.wait_send()
-
-            @pl.when(za == zh)
-            def _():
-                over.wait_send()
-                onward.wait_send()
-
-            for copy in coef_near(i, rb, q) + coef_far(i, rb, q):
+            for copy in coef_z(i, r, rb, q)[1:] + coef_near(i, rb, q) + coef_far(i, rb, q):
                 copy.wait_send()
-
 
     rotations = ((r1, rb1), (r2, rb2))
 
@@ -214,8 +174,6 @@
             r, rb = rotations[i]
             if word[0] == "z":
                 coef_z_start(i, r, rb, q)
-            elif word[0] == "o":
-                coef_onward(i, r, rb, q)
             elif word[0] == "n":
                 coef_near_start(i, r, rb, q)
             else:
@@ -314,7 +272,7 @@
         ).astype(jnp.bfloat16)
         return carry
 
-    own_slot = (x * 2 + zb) * 2 + core
+    own_slot = (x * 2 + core) * 2 + za
     half_lanes = pl.ds(mine, HALF)
 
     def back(j):
@@ -347,13 +305,13 @@
     right, left = device(x_=around(x, 1)), device(x_=around(x, 3))
 
     def slot_at(step, b):
-        return (around(x, step) * 2 + b) * 2 + core
+        return (around(x, step) * 2 + core) * 2 + b
 
     def own_sends(i, g, j):
-        return [send(i, g, own_slot, j, n, to) for n, to in enumerate((device(zb_=1 - zb), right, left, other_core))]
+        return [send(i, g, own_slot, j, n, to) for n, to in enumerate((device(za_=1 - za), right, left, other_core))]
 
     def pair_sends(i, g, j):
-        return [send(i, g, slot_at(0, 1 - zb), j, 4 + n, to) for n, to in enumerate((right, left, other_core))]
+        return [send(i, g, slot_at(0, 1 - za), j, 4 + n, to) for n, to in enumerate((right, left, other_core))]
 
     def near_sends(i, g, j):
         sends = []
@@ -378,7 +336,7 @@
             copy.start()
 
     def gather_pair(i, g, j):
-        arrived(i, g, slot_at(0, 1 - zb), j)
+        arrived(i, g, slot_at(0, 1 - za), j)
         for copy in pair_sends(i, g, j):
             copy.start()
 
@@ -395,7 +353,7 @@
         for copy in far_sends(i, g, j):
             copy.start()
         for slot in range(8):
-            arrived(i, g, slot * 2 + 1 - core, j)
+            arrived(i, g, ((slot // 2) * 2 + 1 - core) * 2 + slot % 2, j)
 
     def gather_end(i, g):
         def step(j, carry):
@@ -416,13 +374,13 @@
         return total
 
     def partial_send(i, j):
-        return remote(pbuf.at[i, j], prec.at[i, j], p_s.at[i, j], p_r.at[i, j], device(za_=1 - za))
+        return remote(pbuf.at[i, j], prec.at[i, j], p_s.at[i, j], p_r.at[i, j], device(zb_=1 - zb))
 
     def multiply(i, g, rb, j):
         gather_far(i, g, j)
-        pbuf[i, j] = product(g, rb, j, 1 - za).astype(jnp.bfloat16)
+        pbuf[i, j] = product(g, rb, j, 1 - zb).astype(jnp.bfloat16)
         partial_send(i, j).start()
-        tq[j] = product(g, rb, j, za)
+        tq[j] = product(g, rb, j, zb)
 
     at("stay")
     for j in range(CHUNKS):
@@ -492,12 +450,12 @@
     def norm_sends():
         sends = [norm_send(own_slot, 0, other_core)]
         for n, (step, b) in enumerate(others):
-            sends.append(norm_send(own_slot, 1 + n, device(x_=around(x, step), zb_=(zb + b) % 2)))
+            sends.append(norm_send(own_slot, 1 + n, device(x_=around(x, step), za_=(za + b) % 2)))
         return sends
 
     def norm_forwards():
         return [
-            norm_send(slot_at(step, (zb + b) % 2), 8 + n, other_core) for n, (step, b) in enumerate(others)
+            norm_send(slot_at(step, (za + b) % 2), 8 + n, other_core) for n, (step, b) in enumerate(others)
         ]
 
     for copy in norm_sends():
@@ -515,7 +473,7 @@
     gather_near(1, g2, 1)
     at("near11")
     for slot in range(8):
-        norm_send(slot * 2 + 1 - core, 0, other_core).wait_recv()
+        norm_send(((slot // 2) * 2 + 1 - core) * 2 + slot % 2, 0, other_core).wait_recv()
 
     def normalize(j):
         def step(slot, carry):
@@ -530,9 +488,9 @@
     def multiply_normed(j):
         gather_far(1, g2, j)
         normalize(j)
-        pbuf[1, j] = product(lhs, rb2, 0, 1 - za).astype(jnp.bfloat16)
+        pbuf[1, j] = product(lhs, rb2, 0, 1 - zb).astype(jnp.bfloat16)
         partial_send(1, j).start()
-        tq[j] = product(lhs, rb2, 0, za)
+        tq[j] = product(lhs, rb2, 0, zb)
 
     def finished(j):
         partial_send(1, j).wait_recv()
@@ -592,7 +550,6 @@
             pltpu.VMEM((16, ROWS, LANES), bf16),
             pltpu.VMEM((2, 4096, LANES), bf16),
             pltpu.VMEM((2, 4096, LANES), bf16),
-            pltpu.VMEM((2, 1024, LANES), bf16),
             pltpu.VMEM((2, CHUNKS, CROWS, LANES), bf16),
             pltpu.VMEM((2, CHUNKS, CROWS, LANES), bf16),
             pltpu.VMEM((CHUNKS, CROWS, LANES), f32),
@@ -607,7 +564,7 @@
             dma((2, CHUNKS)), dma((2, CHUNKS)),
             dma((7,)), dma((7,)),
             dma((15,)), dma((16,)),
-            dma((2, PIECES, 2)), dma((2, PIECES, 2)), dma((2, PIECES)),
+            dma((2, PIECES, 3)), dma((2, PIECES, 4)),
             dma((2, 2, PIECES, 4)), dma((2, 2, PIECES, 4)),
         ],
         compiler_params=pltpu.CompilerParams(

time: 177 us -> 163 us (0.921)
  Pallas kernels: 174 us -> 160 us
    pallas_call x1, Pallas kernels: 174 us -> 160 us  [shards(): pl.pallas_call(kernel, out_shape=jax.ShapeDtypeStruct((ROWS, LANES), bf16...]
where the time goes in v5:
time: 163 us
  Pallas kernels  160 us (98%)
  local copies, waits for them, and re-layouts  3.18 us (2%)
    pallas_call x1, Pallas kernels, shards(): pl.pallas_call(kernel, out_shape=jax.ShapeDtypeStruct((ROWS, LANES), bf16...  160 us

profile of v5, /device:TPU:1, one launch (start us, length us, event | category | flops | bytes accessed | tf_op | source)
XLA Modules:
  0.0 163.0 jit_solution(12831482391557698862)
XLA Ops:
  0.0 1.4 copy.5.pot
  1.4 159.8 %shard_map.46 = bf16[768,256]{1,0:T(8,128)(2,1)} custom-call(bf16[768,256]{1,0:T(8,128)(2,1)} %bitcast.3, bf16[96,64]{1,0:T(8,128)(2,1)} %copy.5.pot, bf16[1024,256]{1,0:T(8,128)(2,1)} %r1.1, bf16[1024,256]{1,0:T(8,128)(2,1)} %r2.1), custom_call_target="tpu_custom_call" | custom-call | tf_op jit(solution)/shard_map/pallas_call | solution.py:537
  161.2 1.8 %copy.7 = bf16[12,64,256]{2,1,0:T(8,128)(2,1)} copy(bf16[12,64,256]{2,1,0:T(8,128)(2,1)} %bitcast.2) | data formatting | bytes 786432

commit v6 on v5

--- a/solution.py
+++ b/solution.py
@@ -35,15 +35,15 @@
 
 
 SCHEDULE = {
-    "start": "z00",
-    "swap": "z01",
-    "rim0": "n00",
-    "back": "n01",
-    "stay": "z10",
+    "start": "z00 z01",
+    "rim0": "z10",
+    "back": "n00",
+    "stay": "n01",
     "own02": "f00 f01",
     "pair02": "z11 n10",
     "mul00": "n11",
-    "turn2": "f10 f11",
+    "share": "f10",
+    "pair11": "f11",
 }
 
 
@@ -425,7 +425,6 @@
     gather_pair(1, g2, 0)
     at("pair10")
     sums = turned(2, sums)
-    at("turn2")
     sq[dom] = sums
 
     def share(step):
@@ -434,6 +433,9 @@
 
     for step in range(1, 8):
         share(step).start()
+    at("share")
+    gather_pair(1, g2, 1)
+    at("pair11")
     for step in range(1, 8):
         share(step).wait_recv()
     total = sq[0]
@@ -461,8 +463,6 @@
     for copy in norm_sends():
         copy.start()
     at("norm")
-    gather_pair(1, g2, 1)
-    at("pair11")
     gather_near(1, g2, 0)
     at("near10")
     gather_pair(1, g2, 2)

time: 163 us -> 151 us (0.926)
  Pallas kernels: 160 us -> 148 us
    pallas_call x1, Pallas kernels: 160 us -> 148 us  [shards(): pl.pallas_call(kernel, out_shape=jax.ShapeDtypeStruct((ROWS, LANES), bf16...]
where the time goes in v6:
time: 151 us
  Pallas kernels  148 us (98%)
  local copies, waits for them, and re-layouts  3.18 us (2%)
    pallas_call x1, Pallas kernels, shards(): pl.pallas_call(kernel, out_shape=jax.ShapeDtypeStruct((ROWS, LANES), bf16...  148 us
    unnamed x2, local copies, waits for them, and re-layouts  3.18 us

profile of v6, /device:TPU:1, one launch (start us, length us, event | category | flops | bytes accessed | tf_op | source)
XLA Modules:
  0.0 151.2 jit_solution(17858344608581153419)
XLA Ops:
  0.0 1.4 copy.5.pot
  1.4 148.0 %shard_map.46 = bf16[768,256]{1,0:T(8,128)(2,1)} custom-call(bf16[768,256]{1,0:T(8,128)(2,1)} %bitcast.3, bf16[96,64]{1,0:T(8,128)(2,1)} %copy.5.pot, bf16[1024,256]{1,0:T(8,128)(2,1)} %r1.1, bf16[1024,256]{1,0:T(8,128)(2,1)} %r2.1), custom_call_target="tpu_custom_call" | custom-call | tf_op jit(solution)/shard_map/pallas_call | solution.py:537
  149.5 1.8 %copy.7 = bf16[12,64,256]{2,1,0:T(8,128)(2,1)} copy(bf16[12,64,256]{2,1,0:T(8,128)(2,1)} %bitcast.2) | data formatting | bytes 786432

commit v7 on v6

--- a/solution.py
+++ b/solution.py
@@ -36,7 +36,7 @@
 
 SCHEDULE = {
     "start": "z00 z01",
-    "rim0": "z10",
+    "first": "z10",
     "back": "n00",
     "stay": "n01",
     "own02": "f00 f01",
@@ -377,7 +377,6 @@
         return remote(pbuf.at[i, j], prec.at[i, j], p_s.at[i, j], p_r.at[i, j], device(zb_=1 - zb))
 
     def multiply(i, g, rb, j):
-        gather_far(i, g, j)
         pbuf[i, j] = product(g, rb, j, 1 - zb).astype(jnp.bfloat16)
         partial_send(i, j).start()
         tq[j] = product(g, rb, j, zb)
@@ -395,11 +394,14 @@
     at("near00")
     gather_near(0, g1, 1)
     at("near01")
+    gather_far(0, g1, 0)
+    gather_near(0, g1, 2)
+    at("near02")
+    gather_far(0, g1, 1)
+    at("far01")
     coef_wait(0, rb1)
     multiply(0, g1, rb1, 0)
     at("mul00")
-    gather_near(0, g1, 2)
-    at("near02")
     multiply(0, g1, rb1, 1)
     at("mul01")
 
@@ -418,6 +420,7 @@
 
     sums = turned(0, jnp.zeros((8, LANES), jnp.float32))
     at("turn0")
+    gather_far(0, g1, 2)
     multiply(0, g1, rb1, 2)
     at("mul02")
     sums = turned(1, sums)
@@ -486,8 +489,6 @@
         lax.fori_loop(0, 16, step, 0)
 
     def multiply_normed(j):
-        gather_far(1, g2, j)
-        normalize(j)
         pbuf[1, j] = product(lhs, rb2, 0, 1 - zb).astype(jnp.bfloat16)
         partial_send(1, j).start()
         tq[j] = product(lhs, rb2, 0, zb)
@@ -504,11 +505,17 @@
 
         lax.fori_loop(0, CROWS // 32, finish, 0)
 
+    gather_far(1, g2, 0)
+    normalize(0)
     coef_wait(1, rb2)
     multiply_normed(0)
     gather_near(1, g2, 2)
+    gather_far(1, g2, 1)
+    normalize(1)
     multiply_normed(1)
     finished(0)
+    gather_far(1, g2, 2)
+    normalize(2)
     multiply_normed(2)
     finished(1)
     finished(2)

time: 151 us -> 150 us (level)
  no operation moved by 1% of the time
where the time goes in v7:
time: 150 us
  Pallas kernels  147 us (98%)
  local copies, waits for them, and re-layouts  3.18 us (2%)
    pallas_call x1, Pallas kernels, shards(): pl.pallas_call(kernel, out_shape=jax.ShapeDtypeStruct((ROWS, LANES), bf16...  147 us
    unnamed x2, local copies, waits for them, and re-layouts  3.18 us

profile of v7, /device:TPU:1, one launch (start us, length us, event | category | flops | bytes accessed | tf_op | source)
XLA Modules:
  0.0 150.2 jit_solution(10119828214096087183)
XLA Ops:
  0.0 1.4 copy.5.pot
  1.4 147.0 %shard_map.46 = bf16[768,256]{1,0:T(8,128)(2,1)} custom-call(bf16[768,256]{1,0:T(8,128)(2,1)} %bitcast.3, bf16[96,64]{1,0:T(8,128)(2,1)} %copy.5.pot, bf16[1024,256]{1,0:T(8,128)(2,1)} %r1.1, bf16[1024,256]{1,0:T(8,128)(2,1)} %r2.1), custom_call_target="tpu_custom_call" | custom-call | tf_op jit(solution)/shard_map/pallas_call | solution.py:544
  148.4 1.8 %copy.7 = bf16[12,64,256]{2,1,0:T(8,128)(2,1)} copy(bf16[12,64,256]{2,1,0:T(8,128)(2,1)} %bitcast.2) | data formatting | bytes 786432

commit v8 on v7

--- a/solution.py
+++ b/solution.py
@@ -221,7 +221,7 @@
             vpad[at, 8:72, :] = value
             return carry
 
-        lax.fori_loop(0, count, step, 0)
+        lax.fori_loop(0, count, step, 0, unroll=3)
 
     def applied(i):
         center = vpad[i + 6, 8:72, :]
@@ -253,7 +253,7 @@
         ).astype(jnp.bfloat16)
         return carry
 
-    lax.fori_loop(0, PAIR, first, 0)
+    lax.fori_loop(0, PAIR, first, 0, unroll=2)
     for copy in rims(1, dext):
         copy.start()
     at("first")
@@ -414,7 +414,7 @@
             g2[own_slot, pl.ds(aligned(j * CROWS + n * 32, 32), 32), :] = value.astype(jnp.bfloat16)
             return total + jnp.sum((value * value).reshape(4, 8, LANES), axis=0)
 
-        sums = lax.fori_loop(0, CROWS // 32, step, sums)
+        sums = lax.fori_loop(0, CROWS // 32, step, sums, unroll=2)
         gather_own(1, g2, j)
         return sums
 
@@ -503,7 +503,7 @@
             ).astype(jnp.bfloat16)
             return carry
 
-        lax.fori_loop(0, CROWS // 32, finish, 0)
+        lax.fori_loop(0, CROWS // 32, finish, 0, unroll=2)
 
     gather_far(1, g2, 0)
     normalize(0)

time: 150 us -> 151 us (level)
  no operation moved by 1% of the time
where the time goes in v8:
time: 151 us; the launch traced here: 150 us
  Pallas kernels  147 us (97%)
  local copies, waits for them, and re-layouts  3.18 us (2%)
    pallas_call x1, Pallas kernels, shards(): pl.pallas_call(kernel, out_shape=jax.ShapeDtypeStruct((ROWS, LANES), bf16...  147 us
    unnamed x2, local copies, waits for them, and re-layouts  3.18 us

profile of v8, /device:TPU:1, one launch (start us, length us, event | category | flops | bytes accessed | tf_op | source)
XLA Modules:
  0.0 150.4 jit_solution(15916161294170462138)
XLA Ops:
  0.0 1.4 copy.5.pot
  1.4 147.2 %shard_map.46 = bf16[768,256]{1,0:T(8,128)(2,1)} custom-call(bf16[768,256]{1,0:T(8,128)(2,1)} %bitcast.3, bf16[96,64]{1,0:T(8,128)(2,1)} %copy.5.pot, bf16[1024,256]{1,0:T(8,128)(2,1)} %r1.1, bf16[1024,256]{1,0:T(8,128)(2,1)} %r2.1), custom_call_target="tpu_custom_call" | custom-call | tf_op jit(solution)/shard_map/pallas_call | solution.py:544
  148.6 1.8 %copy.7 = bf16[12,64,256]{2,1,0:T(8,128)(2,1)} copy(bf16[12,64,256]{2,1,0:T(8,128)(2,1)} %bitcast.2) | data formatting | bytes 786432
